TPU v7x, 128 devices: a whole 4x4x4 slice. The times are simulated.
128 devices in a mesh: frame: 4 (over z_hi, core), vox: 32 (over x, z_lo, y).
Axes of the slice: x: 4, y: 4, z: 4 (z_hi: 2, z_lo: 2; z = z_hi * 2 + z_lo), core: 2. Of those that a mesh axis runs over, the one named last changes fastest.
Arguments:
- echoes: bfloat16 [32, 1024, 2048], P('frame', 'vox'), may hold values from -12 to 12
- delays: int32 [128, 1024], P(None, 'vox'), may hold values from 0 to 1920
- apod: bfloat16 [128, 1024], P(None, 'vox'), may hold values from 0.0099487305 to 0.099609375
- pattern: int32 [128, 32], replicated, may hold values from 0 to 1, as said below
- start_block: float32 [32, 16], replicated, may hold values from -6 to 6
- clutter_rank: int32 [1], replicated, may hold values from 2 to 16
Outputs:
- filtered: float32 [32, 16384], P(None, ('frame', 'vox'))
Inputs may be any that keep to these rules, and one draw needn't show every extreme that they name: Call the blocks b with (b) % 32 == r the blocks of r (4 of them). For every element block c and every r, between 1 and 2 blocks of r have pattern[b, c] = 1; in every draw some r has exactly 2 such blocks for every c.
All inputs are finite; a program needn't handle non-finite values.
Results may differ from a plain program's by a relative error of at most 0.00035.
Values sent between devices are 32-bit elements; how exact they have to be, the bound alone decides.
No kernel may reach another device: no remote copies, remote signals or barrier semaphores. Data moves between devices by JAX's collectives and lax.ppermute only.
A program may use at most 128 MiB of HBM per device.

v0:
```python
import jax
import jax.numpy as jnp
from jax import lax
from jax.sharding import PartitionSpec as P

VB = 128
VOX_DEV = 128


def orthonormal(block):
    columns = []
    for column in range(block.shape[1]):
        vector = block[:, column]
        for earlier in columns:
            vector = vector - jnp.sum(earlier * vector) * earlier
        vector = vector * lax.rsqrt(jnp.sum(vector * vector) + 1e-06)
        columns.append(vector)
    return jnp.stack(columns, axis=1)


def slot_map(marks, slot_count):
    own_blocks = marks.shape[1]
    running = jnp.cumsum(marks, axis=1) - 1
    slots = jnp.arange(slot_count, dtype=jnp.int32)
    hits = (marks[:, None, :] == 1) & (running[:, None, :] == slots[None, :, None])
    places = jnp.arange(own_blocks, dtype=jnp.int32)
    local_block = jnp.sum(jnp.where(hits, places[None, None, :], 0), axis=2)
    valid = jnp.sum(hits.astype(jnp.int32), axis=2)
    return (local_block, valid)


def per_device(echoes, delays, apod, pattern, start_block, clutter_rank):
    n_vox = lax.axis_size("vox")
    n_frame = lax.axis_size("frame")
    vox_index = lax.axis_index("vox")
    f_dev, group_width, samples_total = echoes.shape
    per_span = VOX_DEV // VB
    own_blocks = n_frame * per_span
    slot_count = own_blocks // 2
    by_element = jnp.transpose(echoes, (1, 0, 2))
    column = lax.dynamic_slice_in_dim(pattern, vox_index, 1, 1)[:, 0]
    marks = jnp.transpose(column.reshape(n_frame, n_vox, per_span), (1, 0, 2)).reshape(
        n_vox, own_blocks
    )
    local_block, valid = slot_map(marks, slot_count)
    targets = jnp.arange(n_vox, dtype=jnp.int32)[:, None]
    block_ids = (local_block // per_span * n_vox + targets) * per_span + local_block % per_span

    def element_run(sequence, start):
        return lax.dynamic_slice_in_dim(sequence, start, VB, 1)

    def one_tile(block_id, live):
        delay_row = lax.dynamic_index_in_dim(delays, block_id, 0, keepdims=False)
        weight_row = lax.dynamic_index_in_dim(apod, block_id, 0, keepdims=False)
        samples = jax.vmap(element_run)(by_element, delay_row)
        tile_sum = jnp.einsum("efv,e->fv", samples, weight_row, preferred_element_type=jnp.float32)
        return tile_sum * live.astype(jnp.float32)

    group_size = max(1, n_vox // 8)
    rounds = n_vox // group_size
    grouped_ids = block_ids.reshape(rounds, group_size * slot_count)
    grouped_valid = valid.reshape(rounds, group_size * slot_count)
    tiles = lax.map(lambda pair: jax.vmap(one_tile)(pair[0], pair[1]), (grouped_ids, grouped_valid))
    tiles = tiles.reshape(n_vox, slot_count, f_dev, VB)
    placing = (local_block[..., None] == jnp.arange(own_blocks, dtype=jnp.int32)) & (
        valid[..., None] == 1
    )
    placing = placing.astype(jnp.float32)
    partial_value = jnp.einsum("tsj,tsfv->ftjv", placing, tiles, precision=lax.Precision.HIGHEST)
    partial_value = jnp.transpose(partial_value, (0, 2, 1, 3))
    slab = lax.psum_scatter(partial_value, "vox", scatter_dimension=2, tiled=True).reshape(
        f_dev, n_frame, VOX_DEV
    )
    regrouped = lax.all_to_all(slab, "frame", split_axis=1, concat_axis=0, tiled=True)
    own_image = regrouped.reshape(f_dev * n_frame, VOX_DEV)
    gram_matrix = jnp.dot(own_image, own_image.T, precision=lax.Precision.HIGHEST)
    gram_matrix = lax.psum(gram_matrix, ("frame", "vox"))
    basis = orthonormal(jnp.dot(gram_matrix, start_block, precision=lax.Precision.HIGHEST))
    basis = orthonormal(jnp.dot(gram_matrix, basis, precision=lax.Precision.HIGHEST))
    kept_mask = (jnp.arange(basis.shape[1], dtype=jnp.int32) < clutter_rank[0]).astype(jnp.float32)
    coeffs = jnp.dot(basis.T, own_image, precision=lax.Precision.HIGHEST) * kept_mask[:, None]
    return own_image - jnp.dot(basis, coeffs, precision=lax.Precision.HIGHEST)


def solution(mesh):
    placed = (P("frame", "vox", None), P(None, "vox"), P(None, "vox"), P(), P(), P())
    return jax.shard_map(
        per_device, mesh=mesh, in_specs=placed, out_specs=P(None, ("frame", "vox")), check_vma=False
    )
```

profile of v0, /device:TPU:0, one launch (start us, length us, event | category | flops | bytes accessed | tf_op | source)
XLA Modules:
  0.0 1071.9 jit_solution(16176608739764846859)
XLA Ops:
  7.9 27.8 %copy.32 = bf16[8,32,2048]{0,1,2:T(8,128)(2,1)} copy(bf16[8,32,2048]{2,1,0:T(8,128)(2,1)} %param.8) | data formatting | bytes 2097152 | tf_op args[0]
  36.0 355.8 %while.10 = (s32[]{:T(128)}, f32[8,8,8,128]{3,2,1,0:T(8,128)S(1)}, s32[8,8]{1,0:T(8,128)S(1)}, s32[128,32]{1,0:T(8,128)S(1)}, bf16[32,8,2048]{1,0,2:T(8,128)(2,1...) while((s32[]{:T(128)}, f32[8,8,8,128]{3,2,1,0:T(8,128)S(1)}, s32[8,8]{1,0:T(8,128)S(1)}, ...), condition=%wide.region_4.5_spmd, body=%wide.region_3.4_spmd.sunk | while | flops 534578 | bytes 2731361 | solution.py:63
  36.7 31.5 %gather_fusion.1 = bf16[256,8,128]{1,0,2:T(8,128)(2,1)} fusion(bf16[32,8,2048]{1,0,2:T(8,128)(2,1)} %get-tuple-element.598, s32[256]{0:T(256)S(1)} %reshape.162), kind=kCustom, calls=%fused_computation.2.clone.1 | custom fusion | bytes 1051648 | tf_op jit(solution)/shard_map/while/body/eval_jaxpr/vmap(vmap())/gather | solution.py:50
  68.2 11.4 %copy.51 = bf16[8,32,8,128]{3,1,2,0:T(8,128)(2,1)S(1)} copy(bf16[8,32,8,128]{2,1,0,3:T(8,128)(2,1)} %bitcast.421) | data formatting | bytes 1048576 | tf_op jit(solution)/shard_map/while/body/eval_jaxpr/vmap(vmap())/gather | solution.py:50
  81.1 31.5 %gather_fusion.1 = bf16[256,8,128]{1,0,2:T(8,128)(2,1)} fusion(bf16[32,8,2048]{1,0,2:T(8,128)(2,1)} %get-tuple-element.598, s32[256]{0:T(256)S(1)} %reshape.162), kind=kCustom, calls=%fused_computation.2.clone.1 | custom fusion | bytes 1051648 | tf_op jit(solution)/shard_map/while/body/eval_jaxpr/vmap(vmap())/gather | solution.py:50
  112.7 11.4 %copy.51 = bf16[8,32,8,128]{3,1,2,0:T(8,128)(2,1)S(1)} copy(bf16[8,32,8,128]{2,1,0,3:T(8,128)(2,1)} %bitcast.421) | data formatting | bytes 1048576 | tf_op jit(solution)/shard_map/while/body/eval_jaxpr/vmap(vmap())/gather | solution.py:50
  125.6 31.5 %gather_fusion.1 = bf16[256,8,128]{1,0,2:T(8,128)(2,1)} fusion(bf16[32,8,2048]{1,0,2:T(8,128)(2,1)} %get-tuple-element.598, s32[256]{0:T(256)S(1)} %reshape.162), kind=kCustom, calls=%fused_computation.2.clone.1 | custom fusion | bytes 1051648 | tf_op jit(solution)/shard_map/while/body/eval_jaxpr/vmap(vmap())/gather | solution.py:50
  157.1 11.4 %copy.51 = bf16[8,32,8,128]{3,1,2,0:T(8,128)(2,1)S(1)} copy(bf16[8,32,8,128]{2,1,0,3:T(8,128)(2,1)} %bitcast.421) | data formatting | bytes 1048576 | tf_op jit(solution)/shard_map/while/body/eval_jaxpr/vmap(vmap())/gather | solution.py:50
  170.1 31.5 %gather_fusion.1 = bf16[256,8,128]{1,0,2:T(8,128)(2,1)} fusion(bf16[32,8,2048]{1,0,2:T(8,128)(2,1)} %get-tuple-element.598, s32[256]{0:T(256)S(1)} %reshape.162), kind=kCustom, calls=%fused_computation.2.clone.1 | custom fusion | bytes 1051648 | tf_op jit(solution)/shard_map/while/body/eval_jaxpr/vmap(vmap())/gather | solution.py:50
  201.6 11.4 %copy.51 = bf16[8,32,8,128]{3,1,2,0:T(8,128)(2,1)S(1)} copy(bf16[8,32,8,128]{2,1,0,3:T(8,128)(2,1)} %bitcast.421) | data formatting | bytes 1048576 | tf_op jit(solution)/shard_map/while/body/eval_jaxpr/vmap(vmap())/gather | solution.py:50
  214.5 31.5 %gather_fusion.1 = bf16[256,8,128]{1,0,2:T(8,128)(2,1)} fusion(bf16[32,8,2048]{1,0,2:T(8,128)(2,1)} %get-tuple-element.598, s32[256]{0:T(256)S(1)} %reshape.162), kind=kCustom, calls=%fused_computation.2.clone.1 | custom fusion | bytes 1051648 | tf_op jit(solution)/shard_map/while/body/eval_jaxpr/vmap(vmap())/gather | solution.py:50
  246.0 11.4 %copy.51 = bf16[8,32,8,128]{3,1,2,0:T(8,128)(2,1)S(1)} copy(bf16[8,32,8,128]{2,1,0,3:T(8,128)(2,1)} %bitcast.421) | data formatting | bytes 1048576 | tf_op jit(solution)/shard_map/while/body/eval_jaxpr/vmap(vmap())/gather | solution.py:50
  259.0 31.5 %gather_fusion.1 = bf16[256,8,128]{1,0,2:T(8,128)(2,1)} fusion(bf16[32,8,2048]{1,0,2:T(8,128)(2,1)} %get-tuple-element.598, s32[256]{0:T(256)S(1)} %reshape.162), kind=kCustom, calls=%fused_computation.2.clone.1 | custom fusion | bytes 1051648 | tf_op jit(solution)/shard_map/while/body/eval_jaxpr/vmap(vmap())/gather | solution.py:50
  290.5 11.4 %copy.51 = bf16[8,32,8,128]{3,1,2,0:T(8,128)(2,1)S(1)} copy(bf16[8,32,8,128]{2,1,0,3:T(8,128)(2,1)} %bitcast.421) | data formatting | bytes 1048576 | tf_op jit(solution)/shard_map/while/body/eval_jaxpr/vmap(vmap())/gather | solution.py:50
  303.4 31.5 %gather_fusion.1 = bf16[256,8,128]{1,0,2:T(8,128)(2,1)} fusion(bf16[32,8,2048]{1,0,2:T(8,128)(2,1)} %get-tuple-element.598, s32[256]{0:T(256)S(1)} %reshape.162), kind=kCustom, calls=%fused_computation.2.clone.1 | custom fusion | bytes 1051648 | tf_op jit(solution)/shard_map/while/body/eval_jaxpr/vmap(vmap())/gather | solution.py:50
  334.9 11.4 %copy.51 = bf16[8,32,8,128]{3,1,2,0:T(8,128)(2,1)S(1)} copy(bf16[8,32,8,128]{2,1,0,3:T(8,128)(2,1)} %bitcast.421) | data formatting | bytes 1048576 | tf_op jit(solution)/shard_map/while/body/eval_jaxpr/vmap(vmap())/gather | solution.py:50
  347.9 31.5 %gather_fusion.1 = bf16[256,8,128]{1,0,2:T(8,128)(2,1)} fusion(bf16[32,8,2048]{1,0,2:T(8,128)(2,1)} %get-tuple-element.598, s32[256]{0:T(256)S(1)} %reshape.162), kind=kCustom, calls=%fused_computation.2.clone.1 | custom fusion | bytes 1051648 | tf_op jit(solution)/shard_map/while/body/eval_jaxpr/vmap(vmap())/gather | solution.py:50
  379.4 11.4 %copy.51 = bf16[8,32,8,128]{3,1,2,0:T(8,128)(2,1)S(1)} copy(bf16[8,32,8,128]{2,1,0,3:T(8,128)(2,1)} %bitcast.421) | data formatting | bytes 1048576 | tf_op jit(solution)/shard_map/while/body/eval_jaxpr/vmap(vmap())/gather | solution.py:50
  394.4 161.9 %reduce-scatter.2.cloned.1.call-done = f32[8,4,1,128]{3,0,1,2:T(8,128)} async-done(((f32[8,4,32,128]{3,0,1,2:T(8,128)}), f32[8,4,1,128]{3,0,1,2:T(8,128)}) %reduce-scatter.2.cloned.1.call-update) | async-done | bytes 16400 | tf_op jit(solution)/shard_map/reduce_scatter | solution.py:71
  565.9 62.0 %psum.7 = f32[32,32]{1,0:T(8,128)S(1)} all-reduce(f32[32,32]{1,0:T(8,128)S(1)} %fusion.15), channel_id=1, replica_groups=mesh['frame'=4,'vox'=32] {'frame','vox'}, use_global_device_ids=true, to_apply=%region_6.7 | all-reduce | flops 1024 | bytes 8192 | tf_op jit(solution)/shard_map/psum | solution.py:77
  658.4 14.0 %multiply_reduce_fusion.133 = (f32[]{:T(128)}, f32[]{:T(128)}, f32[]{:T(128)}, f32[]{:T(128)}, f32[]{:T(128)}, /*index=5*/f32[]{:T(128)}, f32[]{:T(128)}, f32[]{...) fusion(f32[32]{0:T(128)S(1)} %get-tuple-element.513, ...), kind=kLoop, calls=%fused_computation.422 | loop fusion | flops 2037 | bytes 3200 | tf_op jit(solution)/shard_map/reduce_sum | solution.py:15
  771.0 75.0 %subtract_multiply_fusion.15 = (f32[32,1]{0,1:T(1,128)S(1)}, f32[32,1]{0,1:T(1,128)S(1)}, f32[32,1]{0,1:T(1,128)S(1)}, f32[32,1]{0,1:T(1,128)S(1)}, f32[32,1]{0,...) fusion(f32[32,1]{0,1:T(1,128)S(1)} %get-tuple-element.534, ...), kind=kLoop, calls=%fused_computation.399 | loop fusion | flops 8160 | bytes 4508 | tf_op jit(solution)/shard_map/mul | solution.py:16
  876.5 14.0 %multiply_reduce_fusion.12 = (f32[]{:T(128)}, f32[]{:T(128)}, f32[]{:T(128)}, f32[]{:T(128)}, f32[]{:T(128)}, /*index=5*/f32[]{:T(128)}, f32[]{:T(128)}, f32[]{:...) fusion(f32[32]{0:T(128)S(1)} %get-tuple-element.407, ...), kind=kLoop, calls=%fused_computation.182 | loop fusion | flops 2037 | bytes 3200 | tf_op jit(solution)/shard_map/reduce_sum | solution.py:15
  989.0 75.0 %subtract_multiply_fusion = (f32[32,1]{0,1:T(1,128)S(1)}, f32[32,1]{0,1:T(1,128)S(1)}, f32[32,1]{0,1:T(1,128)S(1)}, f32[32,1]{0,1:T(1,128)S(1)}, f32[32,1]{0,1:T...) fusion(f32[32,1]{0,1:T(1,128)S(1)} %get-tuple-element.428, ...), kind=kLoop, calls=%fused_computation.159 | loop fusion | flops 8160 | bytes 4508 | tf_op jit(solution)/shard_map/mul | solution.py:16
  (173 shorter events, 263.0 us)
Async XLA Ops:
  6.5 0.7 copy-start
  6.5 29.2 %copy-start.1 = (s32[128,32]{0,1:T(8,128)S(1)}, s32[128,32]{0,1:T(8,128)}, u32[]{:S(2)}) copy-start(s32[128,32]{0,1:T(8,128)} %param.9) | copy-start | bytes 49156
  6.5 29.3 %copy-start.2 = (bf16[128,32]{0,1:T(8,128)(2,1)S(1)}, bf16[128,32]{0,1:T(8,128)(2,1)}, u32[]{:S(2)}) copy-start(bf16[128,32]{0,1:T(8,128)(2,1)} %param.10) | copy-start | bytes 24580
  6.5 549.8 %reduce-scatter.2.cloned.1.call-start = ((), (), s32[]{:S(2)}) async-start(), calls=%async_computation.2 | async-start | bytes 540672 | tf_op jit(solution)/shard_map/reduce_scatter | solution.py:71
  36.0 592.0 %copy-start.3 = (f32[32,16]{0,1:T(8,128)S(1)}, f32[32,16]{0,1:T(8,128)}, u32[]{:S(2)}) copy-start(f32[32,16]{0,1:T(8,128)} %param.12) | copy-start | bytes 6148
  556.3 9.5 all-to-all-start
Sparse Core Ops, SparseCore 0:
  393.9 162.3 reduce-scatter.1
where the time goes:
time: 1080 us; the launch traced here: 1070 us
  other arithmetic  415 us (38%)
  local copies, waits for them, and re-layouts  383 us (35%)
  waiting for transfers between devices  167 us (15%)
  blocking collectives  62 us (6%)
  between operations  35.7 us (3%)
    gather x24, local copies, waits for them, and re-layouts, element_run(): return lax.dynamic_slice_in_dim(sequence, start, VB, 1)  344 us
    reduce_sum x50, other arithmetic, orthonormal(): vector = vector - jnp.sum(earlier * vector) * earlier  234 us
    reduce_scatter x1, waiting for transfers between devices, per_device(): lax.psum_scatter(partial_value, 'vox', scatter_dimension=2, tiled=True)  162 us
    mul x2, other arithmetic, orthonormal(): vector = vector * lax.rsqrt(jnp.sum(vector * vector) + 1e-06)  150 us
    psum x1, blocking collectives, per_device(): gram_matrix = lax.psum(gram_matrix, ('frame', 'vox'))  62 us
    reduce_sum x18, other arithmetic, orthonormal(): vector = vector * lax.rsqrt(jnp.sum(vector * vector) + 1e-06)  30.5 us
    unnamed x9, local copies, waits for them, and re-layouts  28.5 us
  transfers between devices with their start and end apart: 2, of which 2 were waited for; matrix products, arithmetic and copies ran while one was open for 0% of the time, Pallas kernels for 0%

commit v1 on v0

v1 whole, which is shorter than its diff:
```python
import jax
import jax.numpy as jnp
from jax import lax
from jax.experimental import pallas as pl
from jax.experimental.pallas import tpu as pltpu
from jax.sharding import PartitionSpec as P

VB = 128
SLOTS = 2
STEP = 4
HIGHEST = lax.Precision.HIGHEST


def dot(a, b, da, db):
    return lax.dot_general(
        a, b, (((da,), (db,)), ((), ())), precision=HIGHEST, preferred_element_type=jnp.float32
    )


def turned(value, index):
    return jnp.take_along_axis(value, index, axis=1, mode="promise_in_bounds")


def beam_kernel(
    pattern_in, delays_in, apod_in, echoes_in, out,
    raw, tiles, delays, table, marks, rows, row_words, turns, turn_words, rest_wide, weight_wide,
    blocks, places, sems, echo_sems,
):
    f_dev, group, samples = echoes_in.shape
    n_tiles = samples // VB
    tile_rows = group * f_dev
    n_blocks = marks.shape[1]
    n_vox = out.shape[0] // SLOTS
    n_own = n_blocks // n_vox
    column = lax.axis_index("vox")
    copy_delays = pltpu.make_async_copy(delays_in, delays, sems.at[0])
    copy_marks = pltpu.make_async_copy(pattern_in, marks, sems.at[1])
    copy_apod = pltpu.make_async_copy(apod_in, table.at[group : 2 * group], sems.at[2])
    copy_delays.start()
    copy_marks.start()
    copy_apod.start()
    copies = []
    for f in range(f_dev):
        own_rows = pl.ds(f * group, group)
        copies.append(pltpu.make_async_copy(echoes_in.at[f], raw.at[own_rows], echo_sems.at[f]))
        copies[f].start()

    copy_delays.wait()
    element = lax.broadcasted_iota(jnp.int32, delays.shape, 0)
    rows[...] = lax.shift_right_logical(delays[...], 7) * group + element
    put_rows = pltpu.make_async_copy(rows, row_words, sems.at[3])
    put_rows.start()
    turns[...] = (VB - delays[...]) & (VB - 1)
    put_turns = pltpu.make_async_copy(turns, turn_words, sems.at[4])
    put_turns.start()
    table[0:group, :] = (delays[...] & (VB - 1)).astype(table.dtype)

    copy_marks.wait()

    count = jnp.int32(0)
    for r in range(n_vox):
        first = jnp.int32(n_own)
        second = jnp.int32(n_own)
        for i in range(n_own - 1, -1, -1):
            marked = marks[column, i * n_vox + r] == 1
            second = jnp.where(marked, first, second)
            first = jnp.where(marked, i, first)
        blocks[count] = first * n_vox + r
        places[count] = r * SLOTS
        blocks[count + 1] = second * n_vox + r
        places[count + 1] = r * SLOTS + 1
        out[r * SLOTS + 1] = jnp.zeros(out.shape[1:], jnp.float32)
        count = count + jnp.where(second < n_own, 2, 1)
    for i in range(2 * STEP - 1):
        blocks[count + i] = blocks[count - 1]
        places[count + i] = places[count - 1]

    copy_apod.wait()
    lane = lax.broadcasted_iota(jnp.int32, (8, VB), 1)

    block_row = lax.broadcasted_iota(jnp.int32, (n_blocks, VB), 0)

    def spread(s, half):
        for i in range(STEP):
            pick = jnp.where(block_row == blocks[s * STEP + i], 1.0, 0.0).astype(table.dtype)
            wide = jnp.dot(table[...], pick, preferred_element_type=jnp.float32)
            at = pl.ds((half * STEP + i) * group, group)
            rest_wide[at, :] = wide[0:group].astype(jnp.int32)
            weight_wide[at, :] = wide[group : 2 * group]

    spread(0, 0)

    tiles[n_tiles * group : (n_tiles + 1) * group] = jnp.zeros((group, f_dev, VB), jnp.float32)
    to_row = lax.broadcasted_iota(jnp.int32, (tile_rows, tile_rows), 0)
    from_row = lax.broadcasted_iota(jnp.int32, (tile_rows, tile_rows), 1)
    moves = (to_row & (f_dev - 1)) * group + lax.shift_right_logical(to_row, 3) == from_row
    moves = jnp.where(moves, 1.0, 0.0).astype(raw.dtype)
    for f in range(f_dev):
        copies[f].wait()
    for q in range(0, n_tiles, 2):
        pair = jnp.dot(
            moves, raw[:, q * VB : (q + 2) * VB], preferred_element_type=jnp.float32
        )
        for half in range(2):
            tiles[(q + half) * group : (q + half + 1) * group] = pair[
                :, half * VB : (half + 1) * VB
            ].reshape(group, f_dev, VB)

    put_rows.wait()
    put_turns.wait()

    def step(s, carry):
        half = s & 1
        own = [blocks[s * STEP + i] for i in range(STEP)]
        totals = [None] * STEP
        for e in range(group):
            for i in range(STEP):
                row = row_words[e, own[i]]
                at = (half * STEP + i) * group + e
                low = tiles[row]
                high = tiles[row + group]
                rest = rest_wide[pl.ds(at, 1), :]
                weight = weight_wide[pl.ds(at, 1), :]
                mixed = jnp.where(lane >= rest, low, high)
                term = pltpu.roll(mixed, turn_words[e, own[i]], 1) * weight
                totals[i] = term if e == 0 else totals[i] + term
        for i in range(STEP):
            out[places[s * STEP + i]] = totals[i]
        spread(s + 1, 1 - half)
        return carry

    lax.fori_loop(0, (count + STEP - 1) // STEP, step, 0)


def place_kernel(rank, marks, parts, out, kept, picks):
    n_vox = parts.shape[0]
    n_own = out.shape[0]
    r = lax.axis_index("vox")
    kept[...] = jnp.where(
        lax.broadcasted_iota(jnp.int32, kept.shape, 0) < rank[0], jnp.float32(1), jnp.float32(0)
    )
    for c in range(0, n_vox, 8):
        before = jnp.zeros((8, VB), jnp.int32)
        for i in range(n_own):
            mark = turned(marks[c : c + 8, :], jnp.full((8, VB), i * n_vox + r, jnp.int32))
            for s in range(SLOTS):
                hit = (mark == 1) & (before == s)
                picks[i, s, c : c + 8, :] = jnp.where(hit, jnp.float32(1), jnp.float32(0))
            before = before + mark
    for i in range(n_own):
        totals = []
        for s in range(SLOTS):
            for half in range(2):
                total = None
                for c in range(half, n_vox, 2):
                    term = parts[c, s] * picks[i, s, c : c + 1, :]
                    total = term if total is None else total + term
                totals.append(total)
        out[i] = (totals[0] + totals[1]) + (totals[2] + totals[3])


def gram_kernel(*refs):
    received, (image, grams, parts) = refs[:-3], refs[-3:]
    n_frame, n_own, f_dev, _ = parts.shape
    own = lax.axis_index("frame")
    for flip in range(n_frame):
        parts[own ^ flip] = received[flip][...]
    spans = [
        jnp.concatenate([parts[f, i] for f in range(n_frame)], axis=0) for i in range(n_own)
    ]
    wide = jnp.concatenate(spans, axis=1)
    gram = dot(wide, wide, 1, 1)
    packed = jnp.concatenate([gram[f * f_dev : (f + 1) * f_dev] for f in range(n_frame)], axis=1)
    for i in range(grams.shape[0]):
        grams[i] = packed
    for f in range(n_frame):
        image[f * f_dev : (f + 1) * f_dev] = parts[f, own]


def orthonormal_rows(z):
    row = lax.broadcasted_iota(jnp.int32, (z.shape[0], 1), 0)
    for k in range(z.shape[0]):
        current = jnp.broadcast_to(z[k : k + 1], z.shape)
        inner = jnp.sum(z * current, axis=1, keepdims=True)
        scale = lax.rsqrt(jnp.sum(current * current, axis=1, keepdims=True) + 1e-06)
        share = jnp.where(row > k, inner, 0.0) * (scale * scale)
        z = jnp.where(row == k, current * scale, z - share * current)
    return z


def subspace_kernel(grams, image, start, kept, out, square):
    frames = image.shape[0]
    f_dev = grams.shape[1]
    packed = jnp.sum(grams[...], axis=0)
    square[...] = jnp.zeros_like(square)
    for f in range(frames // f_dev):
        square[f * f_dev : (f + 1) * f_dev, 0:frames] = packed[:, f * frames : (f + 1) * frames]
    gram = square[...]
    basis = orthonormal_rows(dot(start[...], gram[0:frames], 1, 0))
    basis = orthonormal_rows(dot(basis, gram, 1, 0))[:, 0:frames]
    own = image[...]
    coeffs = dot(basis, own, 1, 0) * kept[...]
    out[...] = own - dot(basis, coeffs, 0, 0)


def per_device(echoes, delays, apod, pattern, start_block, clutter_rank):
    n_vox = lax.axis_size("vox")
    n_frame = lax.axis_size("frame")
    f_dev, group, samples = echoes.shape
    frames = f_dev * n_frame
    n_blocks = delays.shape[0]
    n_own = n_blocks // n_vox
    n_tiles = samples // VB
    f32, i32 = jnp.float32, jnp.int32
    vmem = pl.BlockSpec(memory_space=pltpu.VMEM)
    smem = pl.BlockSpec(memory_space=pltpu.SMEM)
    hbm = pl.BlockSpec(memory_space=pltpu.HBM)
    params = pltpu.CompilerParams(vmem_limit_bytes=32 * 1024 * 1024)
    all_vmem = pltpu.CompilerParams(vmem_limit_bytes=56 * 1024 * 1024)
    slots = pl.pallas_call(
        beam_kernel,
        out_shape=jax.ShapeDtypeStruct((n_vox * SLOTS, f_dev, VB), f32),
        in_specs=[hbm, hbm, hbm, hbm],
        out_specs=vmem,
        scratch_shapes=[
            pltpu.VMEM((f_dev * group, samples), echoes.dtype),
            pltpu.VMEM(((n_tiles + 1) * group, f_dev, VB), f32),
            pltpu.VMEM((group, n_blocks), i32),
            pltpu.VMEM((2 * group, n_blocks), apod.dtype),
            pltpu.SMEM((pattern.shape[1], n_blocks), i32),
            pltpu.VMEM((group, n_blocks), i32),
            pltpu.SMEM((group, n_blocks), i32),
            pltpu.VMEM((group, n_blocks), i32),
            pltpu.SMEM((group, n_blocks), i32),
            pltpu.VMEM((2 * STEP * group, VB), i32),
            pltpu.VMEM((2 * STEP * group, VB), f32),
            pltpu.SMEM((n_vox * SLOTS + 3 * STEP,), i32),
            pltpu.SMEM((n_vox * SLOTS + 3 * STEP,), i32),
            pltpu.SemaphoreType.DMA((5,)),
            pltpu.SemaphoreType.DMA((f_dev,)),
        ],
        compiler_params=all_vmem,
    )(pattern.T, delays.T, apod.T, echoes)
    slots, later_rank = lax.optimization_barrier((slots, clutter_rank))
    parts = lax.all_to_all(slots, "vox", split_axis=0, concat_axis=0, tiled=True)
    placed, kept = pl.pallas_call(
        place_kernel,
        out_shape=(
            jax.ShapeDtypeStruct((n_own, f_dev, VB), f32),
            jax.ShapeDtypeStruct((start_block.shape[1], VB), f32),
        ),
        in_specs=[smem, vmem, vmem],
        out_specs=(vmem, vmem),
        scratch_shapes=[pltpu.VMEM((n_own, SLOTS, n_vox, VB), f32)],
        compiler_params=params,
    )(later_rank, pattern.T, parts.reshape(n_vox, SLOTS, f_dev, VB))

    def flipped(value, flip):
        return lax.ppermute(value, "frame", [(f, f ^ flip) for f in range(n_frame)])

    across = flipped(placed, 2)
    received = [placed, flipped(placed, 1), across, flipped(across, 1)]
    own_image, grams = pl.pallas_call(
        gram_kernel,
        out_shape=(
            jax.ShapeDtypeStruct((frames, VB), f32),
            jax.ShapeDtypeStruct((n_vox, f_dev, VB), f32),
        ),
        in_specs=[vmem] * n_frame,
        out_specs=(vmem, vmem),
        scratch_shapes=[pltpu.VMEM((n_frame, n_own, f_dev, VB), f32)],
        compiler_params=params,
    )(*received)
    grams = lax.all_to_all(grams, "vox", split_axis=0, concat_axis=0, tiled=True)
    return pl.pallas_call(
        subspace_kernel,
        out_shape=jax.ShapeDtypeStruct((frames, VB), f32),
        in_specs=[vmem, vmem, vmem, vmem],
        out_specs=vmem,
        scratch_shapes=[pltpu.VMEM((VB, VB), f32)],
        compiler_params=params,
    )(grams, own_image, start_block.T, kept)


def solution(mesh):
    placed = (P("frame", "vox", None), P(None, "vox"), P(None, "vox"), P(), P(), P())
    return jax.shard_map(
        per_device, mesh=mesh, in_specs=placed, out_specs=P(None, ("frame", "vox")), check_vma=False
    )
```

time: 1080 us -> 48.9 us (0.05)
  other arithmetic: 415 us -> 0 us
  local copies, waits for them, and re-layouts: 383 us -> 0.01 us
  waiting for transfers between devices: 167 us -> 11.5 us
  blocking collectives: 62 us -> 12.2 us
  between operations: 35.7 us -> 0.7 us
  Pallas kernels: 0 us -> 11.7 us
    gather x40 -> x0, local copies, waits for them, and re-layouts: 353 us -> none  [the longest x24 344 us: element_run(): return lax.dynamic_slice_in_dim(sequence, start, VB, 1)]
    reduce_sum x69 -> x0, other arithmetic: 264 us -> none  [the longest x50 234 us: orthonormal(): vector = vector - jnp.sum(earlier * vector) * earlier]
    reduce_scatter x1 -> x0, waiting for transfers between devices: 162 us -> none  [per_device(): lax.psum_scatter(partial_value, 'vox', scatter_dimension=2, tiled=True)]
    mul x3 -> x0, other arithmetic: 150 us -> none  [the longest x2 150 us: orthonormal(): vector = vector * lax.rsqrt(jnp.sum(vector * vector) + 1e-06)]
    psum x1 -> x0, blocking collectives: 62 us -> none  [per_device(): gram_matrix = lax.psum(gram_matrix, ('frame', 'vox'))]
    unnamed x9 -> x4, local copies, waits for them, and re-layouts: 28.5 us -> 0.01 us
    all_to_all x0 -> x1, blocking collectives: none -> 12.2 us  [per_device(): lax.all_to_all(grams, 'vox', split_axis=0, concat_axis=0, tiled=True)]
    pallas_call x0 -> x4, Pallas kernels: none -> 11.7 us  [the longest x1 7.01 us: per_device(): pl.pallas_call(beam_kernel, out_shape=jax.ShapeDtypeStruct((n_vox * SLOTS...]
  transfers between devices with their start and end apart: 2 -> 4, of which waited for: 2 -> 3; matrix products, arithmetic and copies ran while one was open for 0% -> 0% of each run, Pallas kernels for 0% -> 0%
where the time goes in v1:
time: 48.9 us; the launch traced here: 48.6 us
  starting transfers between devices  12.4 us (25%)
  blocking collectives  12.2 us (25%)
  Pallas kernels  11.7 us (24%)
  waiting for transfers between devices  11.5 us (24%)
  between operations  0.7 us (1%)
    all_to_all x1, blocking collectives, per_device(): lax.all_to_all(grams, 'vox', split_axis=0, concat_axis=0, tiled=True)  12.2 us
    all_to_all x1, starting transfers between devices, per_device(): lax.all_to_all(slots, 'vox', split_axis=0, concat_axis=0, tiled=True)  8.77 us
    all_to_all x1, waiting for transfers between devices, per_device(): lax.all_to_all(slots, 'vox', split_axis=0, concat_axis=0, tiled=True)  8.6 us
    pallas_call x1, Pallas kernels, per_device(): pl.pallas_call(beam_kernel, out_shape=jax.ShapeDtypeStruct((n_vox * SLOTS...  7.01 us
    pallas_call x1, Pallas kernels, per_device(): pl.pallas_call(subspace_kernel, out_shape=jax.ShapeDtypeStruct((frames, V...  4.23 us
    ppermute x3, starting transfers between devices, flipped(): return lax.ppermute(value, 'frame', [(f, f ^ flip) for f in range(n_frame)])  3.67 us
    ppermute x3, waiting for transfers between devices, flipped(): return lax.ppermute(value, 'frame', [(f, f ^ flip) for f in range(n_frame)])  2.9 us
  transfers between devices with their start and end apart: 4, of which 3 were waited for; matrix products, arithmetic and copies ran while one was open for 0% of the time, Pallas kernels for 0%

profile of v1, /device:TPU:0, one launch (start us, length us, event | category | flops | bytes accessed | tf_op | source)
XLA Modules:
  0.0 48.6 jit_solution(6844991583756449132)
XLA Ops:
  0.0 7.0 %shard_map.64 = f32[64,8,128]{2,1,0:T(8,128)} custom-call(s32[32,128]{1,0:T(8,128)} %bitcast.6, s32[32,128]{1,0:T(8,128)} %bitcast.9, bf16[32,128]{1,0:T(8,128)(2,1)} %bitcast.10, bf16[8,32,2048]{2,1,0:T(8,128)(2,1)} %echoes_in.1), custom_call_target="tpu_custom_call" | custom-call | tf_op jit(solution)/shard_map/pallas_call | solution.py:220
  7.0 0.0 copy-start
  7.0 8.8 %all-to-all-start = ((f32[64,8,128]{2,1,0:T(8,128)}), f32[64,8,128]{2,1,0:T(8,128)S(1)}, u32[]{:S(2)}, u32[]{:S(2)}) async-start(f32[64,8,128]{2,1,0:T(8,128)} %shard_map.64), calls=%async_computation | async-start | bytes 524288 | tf_op jit(solution)/shard_map/all_to_all | solution.py:245
  16.5 8.6 %all-to-all-done = f32[64,8,128]{2,1,0:T(8,128)S(1)} async-done(((f32[64,8,128]{2,1,0:T(8,128)}), f32[64,8,128]{2,1,0:T(8,128)S(1)}, u32[]{:S(2)}, u32[]{:S(2)}) %all-to-all-start) | async-done | bytes 262176 | tf_op jit(solution)/shard_map/all_to_all | solution.py:245
  25.1 0.0 copy-done
  25.1 0.2 shard_map.65
  25.2 3.7 %collective-permute-start.1 = (f32[4,8,128]{2,1,0:T(8,128)S(1)}, f32[4,8,128]{2,1,0:T(8,128)S(1)}, u32[]{:S(2)}, u32[]{:S(2)}) collective-permute-start(f32[4,8,128]{2,1,0:T(8,128)S(1)} %get-tuple-element.13.refs_0_), channel_id=1, source_target_pairs={{0,64},{32,96},{64,0},{96,32},{1,65},{33,97},{65,1},{97,33},{2,66}... | collective-permute-start | bytes 49160 | tf_op jit(solution)/shard_map/ppermute | solution.py:259
  28.9 0.0 collective-permute-start
  28.9 1.7 %collective-permute-done.1.refs_2_ = f32[4,8,128]{2,1,0:T(8,128)S(1)} collective-permute-done((f32[4,8,128]{2,1,0:T(8,128)S(1)}, f32[4,8,128]{2,1,0:T(8,128)S(1)}, u32[]{:S(2)}, u32[]{:S(2)}) %collective-permute-start.1) | collective-permute-done | bytes 16416 | tf_op jit(solution)/shard_map/ppermute | solution.py:259
  30.6 0.0 collective-permute-start.2
  30.6 0.0 collective-permute-done.refs_1_
  30.6 1.2 %collective-permute-done.2.refs_3_ = f32[4,8,128]{2,1,0:T(8,128)S(1)} collective-permute-done((f32[4,8,128]{2,1,0:T(8,128)S(1)}, f32[4,8,128]{2,1,0:T(8,128)S(1)}, u32[]{:S(2)}, u32[]{:S(2)}) %collective-permute-start.2) | collective-permute-done | bytes 16416 | tf_op jit(solution)/shard_map/ppermute | solution.py:259
  31.8 0.3 shard_map.66
  32.1 0.0 copy-start.1
  32.1 12.2 %all_to_all.10.grams = f32[32,8,128]{2,1,0:T(8,128)S(1)} all-to-all(f32[32,8,128]{2,1,0:T(8,128)S(1)} %get-tuple-element.14), channel_id=1, replica_groups=mesh['frame'=4,'vox'=32] {'vox'}, dimensions={0} | all-to-all | bytes 262144 | tf_op jit(solution)/shard_map/all_to_all | solution.py:274
  44.3 0.0 copy-done.1
  44.3 4.2 %shard_map.67 = f32[32,128]{1,0:T(8,128)} custom-call(f32[32,8,128]{2,1,0:T(8,128)S(1)} %all_to_all.10.grams, f32[32,128]{1,0:T(8,128)S(1)} %get-tuple-element.15.image, f32[16,32]{1,0:T(8,128)S(1)} %bitcast.8, f32[16,128]{1,0:T(8,128)S(1)} %get-tuple-element.16.kept), custom_call_target="tpu_custom_call" | custom-call | tf_op jit(solution)/shard_map/pallas_call | solution.py:275
Async XLA Ops:
  7.0 18.0 %copy-start = (s32[128,32]{0,1:T(8,128)S(1)}, s32[128,32]{0,1:T(8,128)}, u32[]{:S(2)}) copy-start(s32[128,32]{0,1:T(8,128)} %param.9) | copy-start | bytes 49156
  7.0 18.0 %all-to-all-start = ((f32[64,8,128]{2,1,0:T(8,128)}), f32[64,8,128]{2,1,0:T(8,128)S(1)}, u32[]{:S(2)}, u32[]{:S(2)}) async-start(f32[64,8,128]{2,1,0:T(8,128)} %shard_map.64), calls=%async_computation | async-start | bytes 524288 | tf_op jit(solution)/shard_map/all_to_all | solution.py:245
  25.2 5.4 %collective-permute-start.1 = (f32[4,8,128]{2,1,0:T(8,128)S(1)}, f32[4,8,128]{2,1,0:T(8,128)S(1)}, u32[]{:S(2)}, u32[]{:S(2)}) collective-permute-start(f32[4,8,128]{2,1,0:T(8,128)S(1)} %get-tuple-element.13.refs_0_), channel_id=1, source_target_pairs={{0,64},{32,96},{64,0},{96,32},{1,65},{33,97},{65,1},{97,33},{2,66}... | collective-permute-start | bytes 49160 | tf_op jit(solution)/shard_map/ppermute | solution.py:259
  28.9 1.7 %collective-permute-start = (f32[4,8,128]{2,1,0:T(8,128)S(1)}, f32[4,8,128]{2,1,0:T(8,128)S(1)}, u32[]{:S(2)}, u32[]{:S(2)}) collective-permute-start(f32[4,8,128]{2,1,0:T(8,128)S(1)} %get-tuple-element.13.refs_0_), channel_id=1, source_target_pairs={{0,32},{32,0},{64,96},{96,64},{1,33},{33,1},{65,97},{97,65},{2,34}... | collective-permute-start | bytes 49160 | tf_op jit(solution)/shard_map/ppermute | solution.py:259
  30.6 1.2 %collective-permute-start.2 = (f32[4,8,128]{2,1,0:T(8,128)S(1)}, f32[4,8,128]{2,1,0:T(8,128)S(1)}, u32[]{:S(2)}, u32[]{:S(2)}) collective-permute-start(f32[4,8,128]{2,1,0:T(8,128)S(1)} %collective-permute-done.1.refs_2_), channel_id=1, source_target_pairs={{0,32},{32,0},{64,96},{96,64},{1,33},{33,1},{65,97},{97,65},{2,34}... | collective-permute-start | bytes 49160 | tf_op jit(solution)/shard_map/ppermute | solution.py:259
  32.1 12.2 %copy-start.1 = (f32[32,16]{0,1:T(8,128)S(1)}, f32[32,16]{0,1:T(8,128)}, u32[]{:S(2)}) copy-start(f32[32,16]{0,1:T(8,128)} %param.10) | copy-start | bytes 6148

commit v2 on v1

--- a/solution.py
+++ b/solution.py
@@ -122,7 +122,11 @@
                 rest = rest_wide[pl.ds(at, 1), :]
                 weight = weight_wide[pl.ds(at, 1), :]
                 mixed = jnp.where(lane >= rest, low, high)
-                term = pltpu.roll(mixed, turn_words[e, own[i]], 1) * weight
+                if e % 3 == 0:
+                    mixed = turned(mixed, (lane + rest) & (VB - 1))
+                else:
+                    mixed = pltpu.roll(mixed, turn_words[e, own[i]], 1)
+                term = mixed * weight
                 totals[i] = term if e == 0 else totals[i] + term
         for i in range(STEP):
             out[places[s * STEP + i]] = totals[i]
@@ -177,30 +181,36 @@
         image[f * f_dev : (f + 1) * f_dev] = parts[f, own]
 
 
-def orthonormal_rows(z):
-    row = lax.broadcasted_iota(jnp.int32, (z.shape[0], 1), 0)
-    for k in range(z.shape[0]):
-        current = jnp.broadcast_to(z[k : k + 1], z.shape)
-        inner = jnp.sum(z * current, axis=1, keepdims=True)
-        scale = lax.rsqrt(jnp.sum(current * current, axis=1, keepdims=True) + 1e-06)
-        share = jnp.where(row > k, inner, 0.0) * (scale * scale)
-        z = jnp.where(row == k, current * scale, z - share * current)
-    return z
-
-
-def subspace_kernel(grams, image, start, kept, out, square):
+def orthonormal(columns):
+    count = columns.shape[0]
+    for k in range(count):
+        current = columns[k]
+        scale = lax.rsqrt(jnp.sum(current * current, axis=0, keepdims=True) + 1e-06)
+        for j in range(k + 1, count):
+            inner = jnp.sum(current * columns[j], axis=0, keepdims=True)
+            columns[j] = columns[j] - (inner * (scale * scale)) * current
+        columns[k] = current * scale
+
+
+def subspace_kernel(grams, image, start, kept, out, square, columns):
     frames = image.shape[0]
     f_dev = grams.shape[1]
+    count = columns.shape[0]
     packed = jnp.sum(grams[...], axis=0)
-    square[...] = jnp.zeros_like(square)
     for f in range(frames // f_dev):
-        square[f * f_dev : (f + 1) * f_dev, 0:frames] = packed[:, f * frames : (f + 1) * frames]
+        square[f * f_dev : (f + 1) * f_dev, :] = packed[:, f * frames : (f + 1) * frames]
     gram = square[...]
-    basis = orthonormal_rows(dot(start[...], gram[0:frames], 1, 0))
-    basis = orthonormal_rows(dot(basis, gram, 1, 0))[:, 0:frames]
+    for source in (start, columns):
+        wide = dot(gram, jnp.concatenate([source[k] for k in range(count)], axis=1), 1, 0)
+        for k in range(count):
+            columns[k] = wide[:, k * VB : (k + 1) * VB]
+        orthonormal(columns)
     own = image[...]
-    coeffs = dot(basis, own, 1, 0) * kept[...]
-    out[...] = own - dot(basis, coeffs, 0, 0)
+    left = own
+    for k in range(count):
+        coeffs = jnp.sum(columns[k] * own, axis=0, keepdims=True) * kept[k : k + 1, :]
+        left = left - columns[k] * coeffs
+    out[...] = left
 
 
 def per_device(echoes, delays, apod, pattern, start_block, clutter_rank):
@@ -241,7 +251,8 @@
         ],
         compiler_params=all_vmem,
     )(pattern.T, delays.T, apod.T, echoes)
-    slots, later_rank = lax.optimization_barrier((slots, clutter_rank))
+    slots, later_rank, later_start = lax.optimization_barrier((slots, clutter_rank, start_block))
+    wide_start = jnp.broadcast_to(later_start.T[:, :, None], (start_block.shape[1], frames, VB))
     parts = lax.all_to_all(slots, "vox", split_axis=0, concat_axis=0, tiled=True)
     placed, kept = pl.pallas_call(
         place_kernel,
@@ -277,9 +288,12 @@
         out_shape=jax.ShapeDtypeStruct((frames, VB), f32),
         in_specs=[vmem, vmem, vmem, vmem],
         out_specs=vmem,
-        scratch_shapes=[pltpu.VMEM((VB, VB), f32)],
+        scratch_shapes=[
+            pltpu.VMEM((frames, frames), f32),
+            pltpu.VMEM((start_block.shape[1], frames, VB), f32),
+        ],
         compiler_params=params,
-    )(grams, own_image, start_block.T, kept)
+    )(grams, own_image, wide_start, kept)
 
 
 def solution(mesh):

time: 48.9 us -> 47.1 us (0.963)
  Pallas kernels: 11.7 us -> 9.41 us
    pallas_call x1, Pallas kernels: 4.23 us -> 1.97 us  [per_device(): pl.pallas_call(subspace_kernel, out_shape=jax.ShapeDtypeStruct((frames, V...]
where the time goes in v2:
time: 47.1 us; the launch traced here: 46.7 us
  starting transfers between devices  12.8 us (27%)
  blocking collectives  12.2 us (26%)
  waiting for transfers between devices  11.5 us (24%)
  Pallas kernels  9.41 us (20%)
  between operations  0.71 us (2%)
    all_to_all x1, blocking collectives, per_device(): lax.all_to_all(grams, 'vox', split_axis=0, concat_axis=0, tiled=True)  12.2 us
    all_to_all x1, starting transfers between devices, per_device(): lax.all_to_all(slots, 'vox', split_axis=0, concat_axis=0, tiled=True)  9.11 us
    all_to_all x1, waiting for transfers between devices, per_device(): lax.all_to_all(slots, 'vox', split_axis=0, concat_axis=0, tiled=True)  8.6 us
    pallas_call x1, Pallas kernels, per_device(): pl.pallas_call(beam_kernel, out_shape=jax.ShapeDtypeStruct((n_vox * SLOTS...  6.99 us
    ppermute x3, starting transfers between devices, flipped(): return lax.ppermute(value, 'frame', [(f, f ^ flip) for f in range(n_frame)])  3.67 us
    ppermute x3, waiting for transfers between devices, flipped(): return lax.ppermute(value, 'frame', [(f, f ^ flip) for f in range(n_frame)])  2.9 us
    pallas_call x1, Pallas kernels, per_device(): pl.pallas_call(subspace_kernel, out_shape=jax.ShapeDtypeStruct((frames, V...  1.97 us
  transfers between devices with their start and end apart: 4, of which 3 were waited for; matrix products, arithmetic and copies ran while one was open for 0% of the time, Pallas kernels for 0%

profile of v2, /device:TPU:0, one launch (start us, length us, event | category | flops | bytes accessed | tf_op | source)
XLA Modules:
  0.0 46.7 jit_solution(4751752718563506691)
XLA Ops:
  0.0 7.0 %shard_map.64 = f32[64,8,128]{2,1,0:T(8,128)} custom-call(s32[32,128]{1,0:T(8,128)} %bitcast.6, s32[32,128]{1,0:T(8,128)} %bitcast.8, bf16[32,128]{1,0:T(8,128)(2,1)} %bitcast.9, bf16[8,32,2048]{2,1,0:T(8,128)(2,1)} %echoes_in.1), custom_call_target="tpu_custom_call" | custom-call | tf_op jit(solution)/shard_map/pallas_call | solution.py:230
  7.0 0.0 copy-start
  7.0 9.1 %all-to-all-start = ((f32[64,8,128]{2,1,0:T(8,128)}), f32[64,8,128]{2,1,0:T(8,128)S(1)}, u32[]{:S(2)}, u32[]{:S(2)}) async-start(f32[64,8,128]{2,1,0:T(8,128)} %shard_map.64), calls=%async_computation | async-start | bytes 524288 | tf_op jit(solution)/shard_map/all_to_all | solution.py:256
  16.8 8.6 %all-to-all-done = f32[64,8,128]{2,1,0:T(8,128)S(1)} async-done(((f32[64,8,128]{2,1,0:T(8,128)}), f32[64,8,128]{2,1,0:T(8,128)S(1)}, u32[]{:S(2)}, u32[]{:S(2)}) %all-to-all-start) | async-done | bytes 262176 | tf_op jit(solution)/shard_map/all_to_all | solution.py:256
  25.4 0.0 copy-done
  25.4 0.2 shard_map.65
  25.6 3.7 %collective-permute-start.1 = (f32[4,8,128]{2,1,0:T(8,128)S(1)}, f32[4,8,128]{2,1,0:T(8,128)S(1)}, u32[]{:S(2)}, u32[]{:S(2)}) collective-permute-start(f32[4,8,128]{2,1,0:T(8,128)S(1)} %get-tuple-element.14.refs_0_), channel_id=1, source_target_pairs={{0,64},{32,96},{64,0},{96,32},{1,65},{33,97},{65,1},{97,33},{2,66}... | collective-permute-start | bytes 49160 | tf_op jit(solution)/shard_map/ppermute | solution.py:270
  29.2 0.0 collective-permute-start
  29.2 1.7 %collective-permute-done.1.refs_2_ = f32[4,8,128]{2,1,0:T(8,128)S(1)} collective-permute-done((f32[4,8,128]{2,1,0:T(8,128)S(1)}, f32[4,8,128]{2,1,0:T(8,128)S(1)}, u32[]{:S(2)}, u32[]{:S(2)}) %collective-permute-start.1) | collective-permute-done | bytes 16416 | tf_op jit(solution)/shard_map/ppermute | solution.py:270
  30.9 0.0 collective-permute-start.2
  30.9 0.0 collective-permute-done.refs_1_
  30.9 1.2 %collective-permute-done.2.refs_3_ = f32[4,8,128]{2,1,0:T(8,128)S(1)} collective-permute-done((f32[4,8,128]{2,1,0:T(8,128)S(1)}, f32[4,8,128]{2,1,0:T(8,128)S(1)}, u32[]{:S(2)}, u32[]{:S(2)}) %collective-permute-start.2) | collective-permute-done | bytes 16416 | tf_op jit(solution)/shard_map/ppermute | solution.py:270
  32.1 0.3 shard_map.66
  32.4 0.0 copy-start.1
  32.4 12.2 %all_to_all.10.grams = f32[32,8,128]{2,1,0:T(8,128)S(1)} all-to-all(f32[32,8,128]{2,1,0:T(8,128)S(1)} %get-tuple-element.15), channel_id=1, replica_groups=mesh['frame'=4,'vox'=32] {'vox'}, dimensions={0} | all-to-all | bytes 262144 | tf_op jit(solution)/shard_map/all_to_all | solution.py:285
  44.6 0.0 copy-done.1
  44.6 0.1 broadcast_in_dim.2.start
  44.8 2.0 %shard_map.67 = f32[32,128]{1,0:T(8,128)} custom-call(f32[32,8,128]{2,1,0:T(8,128)S(1)} %all_to_all.10.grams, f32[32,128]{1,0:T(8,128)S(1)} %get-tuple-element.16.image, f32[16,32,128]{2,1,0:T(8,128)S(1)} %broadcast_in_dim.2.start, f32[16,128]{1,0:T(8,128)S(1)} %get-tuple-element.18.kept), custom_call_target="tpu_custom_call" | custom-call | tf_op jit(solution)/shard_map/pallas_call | solution.py:286
Async XLA Ops:
  7.0 18.4 %copy-start = (s32[128,32]{0,1:T(8,128)S(1)}, s32[128,32]{0,1:T(8,128)}, u32[]{:S(2)}) copy-start(s32[128,32]{0,1:T(8,128)} %param.9) | copy-start | bytes 49156
  7.0 18.4 %all-to-all-start = ((f32[64,8,128]{2,1,0:T(8,128)}), f32[64,8,128]{2,1,0:T(8,128)S(1)}, u32[]{:S(2)}, u32[]{:S(2)}) async-start(f32[64,8,128]{2,1,0:T(8,128)} %shard_map.64), calls=%async_computation | async-start | bytes 524288 | tf_op jit(solution)/shard_map/all_to_all | solution.py:256
  25.6 5.4 %collective-permute-start.1 = (f32[4,8,128]{2,1,0:T(8,128)S(1)}, f32[4,8,128]{2,1,0:T(8,128)S(1)}, u32[]{:S(2)}, u32[]{:S(2)}) collective-permute-start(f32[4,8,128]{2,1,0:T(8,128)S(1)} %get-tuple-element.14.refs_0_), channel_id=1, source_target_pairs={{0,64},{32,96},{64,0},{96,32},{1,65},{33,97},{65,1},{97,33},{2,66}... | collective-permute-start | bytes 49160 | tf_op jit(solution)/shard_map/ppermute | solution.py:270
  29.2 1.7 %collective-permute-start = (f32[4,8,128]{2,1,0:T(8,128)S(1)}, f32[4,8,128]{2,1,0:T(8,128)S(1)}, u32[]{:S(2)}, u32[]{:S(2)}) collective-permute-start(f32[4,8,128]{2,1,0:T(8,128)S(1)} %get-tuple-element.14.refs_0_), channel_id=1, source_target_pairs={{0,32},{32,0},{64,96},{96,64},{1,33},{33,1},{65,97},{97,65},{2,34}... | collective-permute-start | bytes 49160 | tf_op jit(solution)/shard_map/ppermute | solution.py:270
  30.9 1.2 %collective-permute-start.2 = (f32[4,8,128]{2,1,0:T(8,128)S(1)}, f32[4,8,128]{2,1,0:T(8,128)S(1)}, u32[]{:S(2)}, u32[]{:S(2)}) collective-permute-start(f32[4,8,128]{2,1,0:T(8,128)S(1)} %collective-permute-done.1.refs_2_), channel_id=1, source_target_pairs={{0,32},{32,0},{64,96},{96,64},{1,33},{33,1},{65,97},{97,65},{2,34}... | collective-permute-start | bytes 49160 | tf_op jit(solution)/shard_map/ppermute | solution.py:270
  32.4 12.2 %copy-start.1 = (f32[32,16]{0,1:T(8,128)S(1)}, f32[32,16]{0,1:T(8,128)}, u32[]{:S(2)}) copy-start(f32[32,16]{0,1:T(8,128)} %param.10) | copy-start | bytes 6148

commit v3 on v2

--- a/solution.py
+++ b/solution.py
@@ -23,7 +23,7 @@
 
 def beam_kernel(
     pattern_in, delays_in, apod_in, echoes_in, out,
-    raw, tiles, delays, table, marks, rows, row_words, turns, turn_words, rest_wide, weight_wide,
+    raw, tiles, delays, apod, marks, rows, row_words, turns, turn_words, weight_wide,
     blocks, places, sems, echo_sems,
 ):
     f_dev, group, samples = echoes_in.shape
@@ -35,27 +35,44 @@
     column = lax.axis_index("vox")
     copy_delays = pltpu.make_async_copy(delays_in, delays, sems.at[0])
     copy_marks = pltpu.make_async_copy(pattern_in, marks, sems.at[1])
-    copy_apod = pltpu.make_async_copy(apod_in, table.at[group : 2 * group], sems.at[2])
+    copy_apod = pltpu.make_async_copy(apod_in, apod, sems.at[2])
     copy_delays.start()
     copy_marks.start()
-    copy_apod.start()
     copies = []
     for f in range(f_dev):
         own_rows = pl.ds(f * group, group)
         copies.append(pltpu.make_async_copy(echoes_in.at[f], raw.at[own_rows], echo_sems.at[f]))
         copies[f].start()
+    copy_apod.start()
+
+    to_row = lax.broadcasted_iota(jnp.int32, (tile_rows, tile_rows), 0)
+    from_row = lax.broadcasted_iota(jnp.int32, (tile_rows, tile_rows), 1)
+    moves = (to_row & (f_dev - 1)) * group + lax.shift_right_logical(to_row, 3) == from_row
+    moves = jnp.where(moves, 1.0, 0.0).astype(raw.dtype)
+    tiles[0:group] = jnp.zeros((group, f_dev, VB), jnp.float32)
 
     copy_delays.wait()
     element = lax.broadcasted_iota(jnp.int32, delays.shape, 0)
-    rows[...] = lax.shift_right_logical(delays[...], 7) * group + element
+    rows[...] = lax.shift_right_logical(delays[...] + (VB - 1), 7) * group + element
+    turns[...] = (VB - (delays[...] & (VB - 1))) & (VB - 1)
     put_rows = pltpu.make_async_copy(rows, row_words, sems.at[3])
+    put_turns = pltpu.make_async_copy(turns, turn_words, sems.at[4])
     put_rows.start()
-    turns[...] = (VB - delays[...]) & (VB - 1)
-    put_turns = pltpu.make_async_copy(turns, turn_words, sems.at[4])
     put_turns.start()
-    table[0:group, :] = (delays[...] & (VB - 1)).astype(table.dtype)
 
     copy_marks.wait()
+    for f in range(f_dev):
+        copies[f].wait()
+    copy_apod.wait()
+
+    for q in range(0, n_tiles, 2):
+        pair = jnp.dot(
+            moves, raw[:, q * VB : (q + 2) * VB], preferred_element_type=jnp.float32
+        )
+        for half in range(2):
+            tiles[(q + half + 1) * group : (q + half + 2) * group] = pair[
+                :, half * VB : (half + 1) * VB
+            ].reshape(group, f_dev, VB)
 
     count = jnp.int32(0)
     for r in range(n_vox):
@@ -75,37 +92,16 @@
         blocks[count + i] = blocks[count - 1]
         places[count + i] = places[count - 1]
 
-    copy_apod.wait()
-    lane = lax.broadcasted_iota(jnp.int32, (8, VB), 1)
-
+    past = VB - lax.broadcasted_iota(jnp.int32, (f_dev, VB), 1)
     block_row = lax.broadcasted_iota(jnp.int32, (n_blocks, VB), 0)
 
     def spread(s, half):
         for i in range(STEP):
-            pick = jnp.where(block_row == blocks[s * STEP + i], 1.0, 0.0).astype(table.dtype)
-            wide = jnp.dot(table[...], pick, preferred_element_type=jnp.float32)
+            pick = jnp.where(block_row == blocks[s * STEP + i], 1.0, 0.0).astype(apod.dtype)
             at = pl.ds((half * STEP + i) * group, group)
-            rest_wide[at, :] = wide[0:group].astype(jnp.int32)
-            weight_wide[at, :] = wide[group : 2 * group]
+            weight_wide[at, :] = jnp.dot(apod[...], pick, preferred_element_type=jnp.float32)
 
     spread(0, 0)
-
-    tiles[n_tiles * group : (n_tiles + 1) * group] = jnp.zeros((group, f_dev, VB), jnp.float32)
-    to_row = lax.broadcasted_iota(jnp.int32, (tile_rows, tile_rows), 0)
-    from_row = lax.broadcasted_iota(jnp.int32, (tile_rows, tile_rows), 1)
-    moves = (to_row & (f_dev - 1)) * group + lax.shift_right_logical(to_row, 3) == from_row
-    moves = jnp.where(moves, 1.0, 0.0).astype(raw.dtype)
-    for f in range(f_dev):
-        copies[f].wait()
-    for q in range(0, n_tiles, 2):
-        pair = jnp.dot(
-            moves, raw[:, q * VB : (q + 2) * VB], preferred_element_type=jnp.float32
-        )
-        for half in range(2):
-            tiles[(q + half) * group : (q + half + 1) * group] = pair[
-                :, half * VB : (half + 1) * VB
-            ].reshape(group, f_dev, VB)
-
     put_rows.wait()
     put_turns.wait()
 
@@ -116,17 +112,10 @@
         for e in range(group):
             for i in range(STEP):
                 row = row_words[e, own[i]]
-                at = (half * STEP + i) * group + e
-                low = tiles[row]
-                high = tiles[row + group]
-                rest = rest_wide[pl.ds(at, 1), :]
-                weight = weight_wide[pl.ds(at, 1), :]
-                mixed = jnp.where(lane >= rest, low, high)
-                if e % 3 == 0:
-                    mixed = turned(mixed, (lane + rest) & (VB - 1))
-                else:
-                    mixed = pltpu.roll(mixed, turn_words[e, own[i]], 1)
-                term = mixed * weight
+                turn = turn_words[e, own[i]]
+                mixed = jnp.where(past <= turn, tiles[row], tiles[row + group])
+                weight = weight_wide[pl.ds((half * STEP + i) * group + e, 1), :]
+                term = pltpu.roll(mixed, turn, 1) * weight
                 totals[i] = term if e == 0 else totals[i] + term
         for i in range(STEP):
             out[places[s * STEP + i]] = totals[i]
@@ -236,13 +225,12 @@
             pltpu.VMEM((f_dev * group, samples), echoes.dtype),
             pltpu.VMEM(((n_tiles + 1) * group, f_dev, VB), f32),
             pltpu.VMEM((group, n_blocks), i32),
-            pltpu.VMEM((2 * group, n_blocks), apod.dtype),
+            pltpu.VMEM((group, n_blocks), apod.dtype),
             pltpu.SMEM((pattern.shape[1], n_blocks), i32),
             pltpu.VMEM((group, n_blocks), i32),
             pltpu.SMEM((group, n_blocks), i32),
             pltpu.VMEM((group, n_blocks), i32),
             pltpu.SMEM((group, n_blocks), i32),
-            pltpu.VMEM((2 * STEP * group, VB), i32),
             pltpu.VMEM((2 * STEP * group, VB), f32),
             pltpu.SMEM((n_vox * SLOTS + 3 * STEP,), i32),
             pltpu.SMEM((n_vox * SLOTS + 3 * STEP,), i32),

time: 47.1 us -> 46.8 us (level)
  no operation moved by 1% of the time
where the time goes in v3:
time: 46.8 us; the launch traced here: 46.7 us
  starting transfers between devices  13.1 us (28%)
  blocking collectives  12.2 us (26%)
  waiting for transfers between devices  11.5 us (25%)
  Pallas kernels  9.08 us (19%)
  between operations  0.71 us (2%)
    all_to_all x1, blocking collectives, per_device(): lax.all_to_all(grams, 'vox', split_axis=0, concat_axis=0, tiled=True)  12.2 us
    all_to_all x1, starting transfers between devices, per_device(): lax.all_to_all(slots, 'vox', split_axis=0, concat_axis=0, tiled=True)  9.4 us
    all_to_all x1, waiting for transfers between devices, per_device(): lax.all_to_all(slots, 'vox', split_axis=0, concat_axis=0, tiled=True)  8.6 us
    pallas_call x1, Pallas kernels, per_device(): pl.pallas_call(beam_kernel, out_shape=jax.ShapeDtypeStruct((n_vox * SLOTS...  6.66 us
    ppermute x3, starting transfers between devices, flipped(): return lax.ppermute(value, 'frame', [(f, f ^ flip) for f in range(n_frame)])  3.67 us
    ppermute x3, waiting for transfers between devices, flipped(): return lax.ppermute(value, 'frame', [(f, f ^ flip) for f in range(n_frame)])  2.9 us
    pallas_call x1, Pallas kernels, per_device(): pl.pallas_call(subspace_kernel, out_shape=jax.ShapeDtypeStruct((frames, V...  1.97 us
  transfers between devices with their start and end apart: 4, of which 3 were waited for; matrix products, arithmetic and copies ran while one was open for 0% of the time, Pallas kernels for 0%

profile of v3, /device:TPU:0, one launch (start us, length us, event | category | flops | bytes accessed | tf_op | source)
XLA Modules:
  0.0 46.7 jit_solution(744636723393361642)
XLA Ops:
  0.0 6.7 %shard_map.64 = f32[64,8,128]{2,1,0:T(8,128)} custom-call(s32[32,128]{1,0:T(8,128)} %bitcast.6, s32[32,128]{1,0:T(8,128)} %bitcast.8, bf16[32,128]{1,0:T(8,128)(2,1)} %bitcast.9, bf16[8,32,2048]{2,1,0:T(8,128)(2,1)} %echoes_in.1), custom_call_target="tpu_custom_call" | custom-call | tf_op jit(solution)/shard_map/pallas_call | solution.py:219
  6.7 0.0 copy-start
  6.7 9.4 %all-to-all-start = ((f32[64,8,128]{2,1,0:T(8,128)}), f32[64,8,128]{2,1,0:T(8,128)S(1)}, u32[]{:S(2)}, u32[]{:S(2)}) async-start(f32[64,8,128]{2,1,0:T(8,128)} %shard_map.64), calls=%async_computation | async-start | bytes 524288 | tf_op jit(solution)/shard_map/all_to_all | solution.py:244
  16.7 8.6 %all-to-all-done = f32[64,8,128]{2,1,0:T(8,128)S(1)} async-done(((f32[64,8,128]{2,1,0:T(8,128)}), f32[64,8,128]{2,1,0:T(8,128)S(1)}, u32[]{:S(2)}, u32[]{:S(2)}) %all-to-all-start) | async-done | bytes 262176 | tf_op jit(solution)/shard_map/all_to_all | solution.py:244
  25.3 0.0 copy-done
  25.3 0.2 shard_map.65
  25.5 3.7 %collective-permute-start.1 = (f32[4,8,128]{2,1,0:T(8,128)S(1)}, f32[4,8,128]{2,1,0:T(8,128)S(1)}, u32[]{:S(2)}, u32[]{:S(2)}) collective-permute-start(f32[4,8,128]{2,1,0:T(8,128)S(1)} %get-tuple-element.14.refs_0_), channel_id=1, source_target_pairs={{0,64},{32,96},{64,0},{96,32},{1,65},{33,97},{65,1},{97,33},{2,66}... | collective-permute-start | bytes 49160 | tf_op jit(solution)/shard_map/ppermute | solution.py:258
  29.2 0.0 collective-permute-start
  29.2 1.7 %collective-permute-done.1.refs_2_ = f32[4,8,128]{2,1,0:T(8,128)S(1)} collective-permute-done((f32[4,8,128]{2,1,0:T(8,128)S(1)}, f32[4,8,128]{2,1,0:T(8,128)S(1)}, u32[]{:S(2)}, u32[]{:S(2)}) %collective-permute-start.1) | collective-permute-done | bytes 16416 | tf_op jit(solution)/shard_map/ppermute | solution.py:258
  30.9 0.0 collective-permute-start.2
  30.9 0.0 collective-permute-done.refs_1_
  30.9 1.2 %collective-permute-done.2.refs_3_ = f32[4,8,128]{2,1,0:T(8,128)S(1)} collective-permute-done((f32[4,8,128]{2,1,0:T(8,128)S(1)}, f32[4,8,128]{2,1,0:T(8,128)S(1)}, u32[]{:S(2)}, u32[]{:S(2)}) %collective-permute-start.2) | collective-permute-done | bytes 16416 | tf_op jit(solution)/shard_map/ppermute | solution.py:258
  32.1 0.3 shard_map.66
  32.4 0.0 copy-start.1
  32.4 12.2 %all_to_all.10.grams = f32[32,8,128]{2,1,0:T(8,128)S(1)} all-to-all(f32[32,8,128]{2,1,0:T(8,128)S(1)} %get-tuple-element.15), channel_id=1, replica_groups=mesh['frame'=4,'vox'=32] {'vox'}, dimensions={0} | all-to-all | bytes 262144 | tf_op jit(solution)/shard_map/all_to_all | solution.py:273
  44.6 0.0 copy-done.1
  44.6 0.1 broadcast_in_dim.2.start
  44.7 2.0 %shard_map.67 = f32[32,128]{1,0:T(8,128)} custom-call(f32[32,8,128]{2,1,0:T(8,128)S(1)} %all_to_all.10.grams, f32[32,128]{1,0:T(8,128)S(1)} %get-tuple-element.16.image, f32[16,32,128]{2,1,0:T(8,128)S(1)} %broadcast_in_dim.2.start, f32[16,128]{1,0:T(8,128)S(1)} %get-tuple-element.18.kept), custom_call_target="tpu_custom_call" | custom-call | tf_op jit(solution)/shard_map/pallas_call | solution.py:274
Async XLA Ops:
  6.7 18.7 %copy-start = (s32[128,32]{0,1:T(8,128)S(1)}, s32[128,32]{0,1:T(8,128)}, u32[]{:S(2)}) copy-start(s32[128,32]{0,1:T(8,128)} %param.9) | copy-start | bytes 49156
  6.7 18.7 %all-to-all-start = ((f32[64,8,128]{2,1,0:T(8,128)}), f32[64,8,128]{2,1,0:T(8,128)S(1)}, u32[]{:S(2)}, u32[]{:S(2)}) async-start(f32[64,8,128]{2,1,0:T(8,128)} %shard_map.64), calls=%async_computation | async-start | bytes 524288 | tf_op jit(solution)/shard_map/all_to_all | solution.py:244
  25.5 5.4 %collective-permute-start.1 = (f32[4,8,128]{2,1,0:T(8,128)S(1)}, f32[4,8,128]{2,1,0:T(8,128)S(1)}, u32[]{:S(2)}, u32[]{:S(2)}) collective-permute-start(f32[4,8,128]{2,1,0:T(8,128)S(1)} %get-tuple-element.14.refs_0_), channel_id=1, source_target_pairs={{0,64},{32,96},{64,0},{96,32},{1,65},{33,97},{65,1},{97,33},{2,66}... | collective-permute-start | bytes 49160 | tf_op jit(solution)/shard_map/ppermute | solution.py:258
  29.2 1.7 %collective-permute-start = (f32[4,8,128]{2,1,0:T(8,128)S(1)}, f32[4,8,128]{2,1,0:T(8,128)S(1)}, u32[]{:S(2)}, u32[]{:S(2)}) collective-permute-start(f32[4,8,128]{2,1,0:T(8,128)S(1)} %get-tuple-element.14.refs_0_), channel_id=1, source_target_pairs={{0,32},{32,0},{64,96},{96,64},{1,33},{33,1},{65,97},{97,65},{2,34}... | collective-permute-start | bytes 49160 | tf_op jit(solution)/shard_map/ppermute | solution.py:258
  30.9 1.2 %collective-permute-start.2 = (f32[4,8,128]{2,1,0:T(8,128)S(1)}, f32[4,8,128]{2,1,0:T(8,128)S(1)}, u32[]{:S(2)}, u32[]{:S(2)}) collective-permute-start(f32[4,8,128]{2,1,0:T(8,128)S(1)} %collective-permute-done.1.refs_2_), channel_id=1, source_target_pairs={{0,32},{32,0},{64,96},{96,64},{1,33},{33,1},{65,97},{97,65},{2,34}... | collective-permute-start | bytes 49160 | tf_op jit(solution)/shard_map/ppermute | solution.py:258
  32.4 12.2 %copy-start.1 = (f32[32,16]{0,1:T(8,128)S(1)}, f32[32,16]{0,1:T(8,128)}, u32[]{:S(2)}) copy-start(f32[32,16]{0,1:T(8,128)} %param.10) | copy-start | bytes 6148

commit v4 on v3

--- a/solution.py
+++ b/solution.py
@@ -7,7 +7,7 @@
 
 VB = 128
 SLOTS = 2
-STEP = 4
+STEP = 8
 HIGHEST = lax.Precision.HIGHEST
 
 
@@ -39,10 +39,10 @@
     copy_delays.start()
     copy_marks.start()
     copies = []
-    for f in range(f_dev):
-        own_rows = pl.ds(f * group, group)
-        copies.append(pltpu.make_async_copy(echoes_in.at[f], raw.at[own_rows], echo_sems.at[f]))
-        copies[f].start()
+    for part in range(2):
+        own = pl.ds(part * (f_dev // 2), f_dev // 2)
+        copies.append(pltpu.make_async_copy(echoes_in.at[own], raw.at[own], echo_sems.at[part]))
+        copies[part].start()
     copy_apod.start()
 
     to_row = lax.broadcasted_iota(jnp.int32, (tile_rows, tile_rows), 0)
@@ -61,19 +61,6 @@
     put_turns.start()
 
     copy_marks.wait()
-    for f in range(f_dev):
-        copies[f].wait()
-    copy_apod.wait()
-
-    for q in range(0, n_tiles, 2):
-        pair = jnp.dot(
-            moves, raw[:, q * VB : (q + 2) * VB], preferred_element_type=jnp.float32
-        )
-        for half in range(2):
-            tiles[(q + half + 1) * group : (q + half + 2) * group] = pair[
-                :, half * VB : (half + 1) * VB
-            ].reshape(group, f_dev, VB)
-
     count = jnp.int32(0)
     for r in range(n_vox):
         first = jnp.int32(n_own)
@@ -101,7 +88,19 @@
             at = pl.ds((half * STEP + i) * group, group)
             weight_wide[at, :] = jnp.dot(apod[...], pick, preferred_element_type=jnp.float32)
 
+    copy_apod.wait()
     spread(0, 0)
+    for copy in copies:
+        copy.wait()
+
+    for q in range(0, n_tiles, 2):
+        pair = raw[:, :, q * VB : (q + 2) * VB].reshape(tile_rows, 2 * VB)
+        pair = jnp.dot(moves, pair, preferred_element_type=jnp.float32)
+        for half in range(2):
+            tiles[(q + half + 1) * group : (q + half + 2) * group] = pair[
+                :, half * VB : (half + 1) * VB
+            ].reshape(group, f_dev, VB)
+
     put_rows.wait()
     put_turns.wait()
 
@@ -222,7 +221,7 @@
         in_specs=[hbm, hbm, hbm, hbm],
         out_specs=vmem,
         scratch_shapes=[
-            pltpu.VMEM((f_dev * group, samples), echoes.dtype),
+            pltpu.VMEM(echoes.shape, echoes.dtype),
             pltpu.VMEM(((n_tiles + 1) * group, f_dev, VB), f32),
             pltpu.VMEM((group, n_blocks), i32),
             pltpu.VMEM((group, n_blocks), apod.dtype),
@@ -235,7 +234,7 @@
             pltpu.SMEM((n_vox * SLOTS + 3 * STEP,), i32),
             pltpu.SMEM((n_vox * SLOTS + 3 * STEP,), i32),
             pltpu.SemaphoreType.DMA((5,)),
-            pltpu.SemaphoreType.DMA((f_dev,)),
+            pltpu.SemaphoreType.DMA((2,)),
         ],
         compiler_params=all_vmem,
     )(pattern.T, delays.T, apod.T, echoes)

time: 46.8 us -> 46.7 us (level)
  no operation moved by 1% of the time
where the time goes in v4:
time: 46.7 us; the launch traced here: 46.2 us
  starting transfers between devices  12.8 us (27%)
  blocking collectives  12.2 us (26%)
  waiting for transfers between devices  11.5 us (25%)
  Pallas kernels  8.91 us (19%)
  between operations  0.71 us (2%)
    all_to_all x1, blocking collectives, per_device(): lax.all_to_all(grams, 'vox', split_axis=0, concat_axis=0, tiled=True)  12.2 us
    all_to_all x1, starting transfers between devices, per_device(): lax.all_to_all(slots, 'vox', split_axis=0, concat_axis=0, tiled=True)  9.11 us
    all_to_all x1, waiting for transfers between devices, per_device(): lax.all_to_all(slots, 'vox', split_axis=0, concat_axis=0, tiled=True)  8.6 us
    pallas_call x1, Pallas kernels, per_device(): pl.pallas_call(beam_kernel, out_shape=jax.ShapeDtypeStruct((n_vox * SLOTS...  6.49 us
    ppermute x3, starting transfers between devices, flipped(): return lax.ppermute(value, 'frame', [(f, f ^ flip) for f in range(n_frame)])  3.67 us
    ppermute x3, waiting for transfers between devices, flipped(): return lax.ppermute(value, 'frame', [(f, f ^ flip) for f in range(n_frame)])  2.9 us
    pallas_call x1, Pallas kernels, per_device(): pl.pallas_call(subspace_kernel, out_shape=jax.ShapeDtypeStruct((frames, V...  1.97 us
  transfers between devices with their start and end apart: 4, of which 3 were waited for; matrix products, arithmetic and copies ran while one was open for 0% of the time, Pallas kernels for 0%

profile of v4, /device:TPU:0, one launch (start us, length us, event | category | flops | bytes accessed | tf_op | source)
XLA Modules:
  0.0 46.2 jit_solution(13706331538857435438)
XLA Ops:
  0.0 6.5 %shard_map.64 = f32[64,8,128]{2,1,0:T(8,128)} custom-call(s32[32,128]{1,0:T(8,128)} %bitcast.6, s32[32,128]{1,0:T(8,128)} %bitcast.8, bf16[32,128]{1,0:T(8,128)(2,1)} %bitcast.9, bf16[8,32,2048]{2,1,0:T(8,128)(2,1)} %echoes_in.1), custom_call_target="tpu_custom_call" | custom-call | tf_op jit(solution)/shard_map/pallas_call | solution.py:218
  6.5 0.0 copy-start
  6.5 9.1 %all-to-all-start = ((f32[64,8,128]{2,1,0:T(8,128)}), f32[64,8,128]{2,1,0:T(8,128)S(1)}, u32[]{:S(2)}, u32[]{:S(2)}) async-start(f32[64,8,128]{2,1,0:T(8,128)} %shard_map.64), calls=%async_computation | async-start | bytes 524288 | tf_op jit(solution)/shard_map/all_to_all | solution.py:243
  16.3 8.6 %all-to-all-done = f32[64,8,128]{2,1,0:T(8,128)S(1)} async-done(((f32[64,8,128]{2,1,0:T(8,128)}), f32[64,8,128]{2,1,0:T(8,128)S(1)}, u32[]{:S(2)}, u32[]{:S(2)}) %all-to-all-start) | async-done | bytes 262176 | tf_op jit(solution)/shard_map/all_to_all | solution.py:243
  24.9 0.0 copy-done
  24.9 0.2 shard_map.65
  25.1 3.7 %collective-permute-start.1 = (f32[4,8,128]{2,1,0:T(8,128)S(1)}, f32[4,8,128]{2,1,0:T(8,128)S(1)}, u32[]{:S(2)}, u32[]{:S(2)}) collective-permute-start(f32[4,8,128]{2,1,0:T(8,128)S(1)} %get-tuple-element.14.refs_0_), channel_id=1, source_target_pairs={{0,64},{32,96},{64,0},{96,32},{1,65},{33,97},{65,1},{97,33},{2,66}... | collective-permute-start | bytes 49160 | tf_op jit(solution)/shard_map/ppermute | solution.py:257
  28.7 0.0 collective-permute-start
  28.7 1.7 %collective-permute-done.1.refs_2_ = f32[4,8,128]{2,1,0:T(8,128)S(1)} collective-permute-done((f32[4,8,128]{2,1,0:T(8,128)S(1)}, f32[4,8,128]{2,1,0:T(8,128)S(1)}, u32[]{:S(2)}, u32[]{:S(2)}) %collective-permute-start.1) | collective-permute-done | bytes 16416 | tf_op jit(solution)/shard_map/ppermute | solution.py:257
  30.4 0.0 collective-permute-start.2
  30.4 0.0 collective-permute-done.refs_1_
  30.4 1.2 %collective-permute-done.2.refs_3_ = f32[4,8,128]{2,1,0:T(8,128)S(1)} collective-permute-done((f32[4,8,128]{2,1,0:T(8,128)S(1)}, f32[4,8,128]{2,1,0:T(8,128)S(1)}, u32[]{:S(2)}, u32[]{:S(2)}) %collective-permute-start.2) | collective-permute-done | bytes 16416 | tf_op jit(solution)/shard_map/ppermute | solution.py:257
  31.6 0.3 shard_map.66
  31.9 0.0 copy-start.1
  31.9 12.2 %all_to_all.10.grams = f32[32,8,128]{2,1,0:T(8,128)S(1)} all-to-all(f32[32,8,128]{2,1,0:T(8,128)S(1)} %get-tuple-element.15), channel_id=1, replica_groups=mesh['frame'=4,'vox'=32] {'vox'}, dimensions={0} | all-to-all | bytes 262144 | tf_op jit(solution)/shard_map/all_to_all | solution.py:272
  44.1 0.0 copy-done.1
  44.1 0.1 broadcast_in_dim.2.start
  44.3 2.0 %shard_map.67 = f32[32,128]{1,0:T(8,128)} custom-call(f32[32,8,128]{2,1,0:T(8,128)S(1)} %all_to_all.10.grams, f32[32,128]{1,0:T(8,128)S(1)} %get-tuple-element.16.image, f32[16,32,128]{2,1,0:T(8,128)S(1)} %broadcast_in_dim.2.start, f32[16,128]{1,0:T(8,128)S(1)} %get-tuple-element.18.kept), custom_call_target="tpu_custom_call" | custom-call | tf_op jit(solution)/shard_map/pallas_call | solution.py:273
Async XLA Ops:
  6.5 18.4 %copy-start = (s32[128,32]{0,1:T(8,128)S(1)}, s32[128,32]{0,1:T(8,128)}, u32[]{:S(2)}) copy-start(s32[128,32]{0,1:T(8,128)} %param.9) | copy-start | bytes 49156
  6.5 18.4 %all-to-all-start = ((f32[64,8,128]{2,1,0:T(8,128)}), f32[64,8,128]{2,1,0:T(8,128)S(1)}, u32[]{:S(2)}, u32[]{:S(2)}) async-start(f32[64,8,128]{2,1,0:T(8,128)} %shard_map.64), calls=%async_computation | async-start | bytes 524288 | tf_op jit(solution)/shard_map/all_to_all | solution.py:243
  25.1 5.4 %collective-permute-start.1 = (f32[4,8,128]{2,1,0:T(8,128)S(1)}, f32[4,8,128]{2,1,0:T(8,128)S(1)}, u32[]{:S(2)}, u32[]{:S(2)}) collective-permute-start(f32[4,8,128]{2,1,0:T(8,128)S(1)} %get-tuple-element.14.refs_0_), channel_id=1, source_target_pairs={{0,64},{32,96},{64,0},{96,32},{1,65},{33,97},{65,1},{97,33},{2,66}... | collective-permute-start | bytes 49160 | tf_op jit(solution)/shard_map/ppermute | solution.py:257
  28.7 1.7 %collective-permute-start = (f32[4,8,128]{2,1,0:T(8,128)S(1)}, f32[4,8,128]{2,1,0:T(8,128)S(1)}, u32[]{:S(2)}, u32[]{:S(2)}) collective-permute-start(f32[4,8,128]{2,1,0:T(8,128)S(1)} %get-tuple-element.14.refs_0_), channel_id=1, source_target_pairs={{0,32},{32,0},{64,96},{96,64},{1,33},{33,1},{65,97},{97,65},{2,34}... | collective-permute-start | bytes 49160 | tf_op jit(solution)/shard_map/ppermute | solution.py:257
  30.4 1.2 %collective-permute-start.2 = (f32[4,8,128]{2,1,0:T(8,128)S(1)}, f32[4,8,128]{2,1,0:T(8,128)S(1)}, u32[]{:S(2)}, u32[]{:S(2)}) collective-permute-start(f32[4,8,128]{2,1,0:T(8,128)S(1)} %collective-permute-done.1.refs_2_), channel_id=1, source_target_pairs={{0,32},{32,0},{64,96},{96,64},{1,33},{33,1},{65,97},{97,65},{2,34}... | collective-permute-start | bytes 49160 | tf_op jit(solution)/shard_map/ppermute | solution.py:257
  31.9 12.2 %copy-start.1 = (f32[32,16]{0,1:T(8,128)S(1)}, f32[32,16]{0,1:T(8,128)}, u32[]{:S(2)}) copy-start(f32[32,16]{0,1:T(8,128)} %param.10) | copy-start | bytes 6148

commit v5 on v4

--- a/solution.py
+++ b/solution.py
@@ -33,8 +33,10 @@
     n_vox = out.shape[0] // SLOTS
     n_own = n_blocks // n_vox
     column = lax.axis_index("vox")
+    near_row = lax.rem(column, 8)
     copy_delays = pltpu.make_async_copy(delays_in, delays, sems.at[0])
-    copy_marks = pltpu.make_async_copy(pattern_in, marks, sems.at[1])
+    near = pl.ds(pl.multiple_of((column // 8) * 8, 8), 8)
+    copy_marks = pltpu.make_async_copy(pattern_in.at[near], marks, sems.at[1])
     copy_apod = pltpu.make_async_copy(apod_in, apod, sems.at[2])
     copy_delays.start()
     copy_marks.start()
@@ -60,13 +62,24 @@
     put_rows.start()
     put_turns.start()
 
+    for copy in copies:
+        copy.wait()
+
+    for q in range(0, n_tiles, 2):
+        pair = raw[:, :, q * VB : (q + 2) * VB].reshape(tile_rows, 2 * VB)
+        pair = jnp.dot(moves, pair, preferred_element_type=jnp.float32)
+        for half in range(2):
+            tiles[(q + half + 1) * group : (q + half + 2) * group] = pair[
+                :, half * VB : (half + 1) * VB
+            ].reshape(group, f_dev, VB)
+
     copy_marks.wait()
     count = jnp.int32(0)
     for r in range(n_vox):
         first = jnp.int32(n_own)
         second = jnp.int32(n_own)
         for i in range(n_own - 1, -1, -1):
-            marked = marks[column, i * n_vox + r] == 1
+            marked = marks[near_row, i * n_vox + r] == 1
             second = jnp.where(marked, first, second)
             first = jnp.where(marked, i, first)
         blocks[count] = first * n_vox + r
@@ -90,17 +103,6 @@
 
     copy_apod.wait()
     spread(0, 0)
-    for copy in copies:
-        copy.wait()
-
-    for q in range(0, n_tiles, 2):
-        pair = raw[:, :, q * VB : (q + 2) * VB].reshape(tile_rows, 2 * VB)
-        pair = jnp.dot(moves, pair, preferred_element_type=jnp.float32)
-        for half in range(2):
-            tiles[(q + half + 1) * group : (q + half + 2) * group] = pair[
-                :, half * VB : (half + 1) * VB
-            ].reshape(group, f_dev, VB)
-
     put_rows.wait()
     put_turns.wait()
 
@@ -225,7 +227,7 @@
             pltpu.VMEM(((n_tiles + 1) * group, f_dev, VB), f32),
             pltpu.VMEM((group, n_blocks), i32),
             pltpu.VMEM((group, n_blocks), apod.dtype),
-            pltpu.SMEM((pattern.shape[1], n_blocks), i32),
+            pltpu.SMEM((8, n_blocks), i32),
             pltpu.VMEM((group, n_blocks), i32),
             pltpu.SMEM((group, n_blocks), i32),
             pltpu.VMEM((group, n_blocks), i32),

time: 46.7 us -> 46.9 us (level)
  Pallas kernels: 8.91 us -> 9.69 us
  starting transfers between devices: 12.8 us -> 12.3 us
    pallas_call x1, Pallas kernels: 6.49 us -> 7.26 us  [per_device(): pl.pallas_call(beam_kernel, out_shape=jax.ShapeDtypeStruct((n_vox * SLOTS...]
    all_to_all x1, starting transfers between devices: 9.11 us -> 8.59 us  [per_device(): lax.all_to_all(slots, 'vox', split_axis=0, concat_axis=0, tiled=True)]
where the time goes in v5:
time: 46.9 us; the launch traced here: 46.5 us
  starting transfers between devices  12.3 us (26%)
  blocking collectives  12.2 us (26%)
  waiting for transfers between devices  11.5 us (25%)
  Pallas kernels  9.69 us (21%)
  between operations  0.71 us (2%)
    all_to_all x1, blocking collectives, per_device(): lax.all_to_all(grams, 'vox', split_axis=0, concat_axis=0, tiled=True)  12.2 us
    all_to_all x1, waiting for transfers between devices, per_device(): lax.all_to_all(slots, 'vox', split_axis=0, concat_axis=0, tiled=True)  8.6 us
    all_to_all x1, starting transfers between devices, per_device(): lax.all_to_all(slots, 'vox', split_axis=0, concat_axis=0, tiled=True)  8.59 us
    pallas_call x1, Pallas kernels, per_device(): pl.pallas_call(beam_kernel, out_shape=jax.ShapeDtypeStruct((n_vox * SLOTS...  7.26 us
    ppermute x3, starting transfers between devices, flipped(): return lax.ppermute(value, 'frame', [(f, f ^ flip) for f in range(n_frame)])  3.67 us
    ppermute x3, waiting for transfers between devices, flipped(): return lax.ppermute(value, 'frame', [(f, f ^ flip) for f in range(n_frame)])  2.9 us
    pallas_call x1, Pallas kernels, per_device(): pl.pallas_call(subspace_kernel, out_shape=jax.ShapeDtypeStruct((frames, V...  1.98 us
  transfers between devices with their start and end apart: 4, of which 3 were waited for; matrix products, arithmetic and copies ran while one was open for 0% of the time, Pallas kernels for 0%

profile of v5, /device:TPU:0, one launch (start us, length us, event | category | flops | bytes accessed | tf_op | source)
XLA Modules:
  0.0 46.5 jit_solution(1063787103023808376)
XLA Ops:
  0.0 7.3 %shard_map.64 = f32[64,8,128]{2,1,0:T(8,128)} custom-call(s32[32,128]{1,0:T(8,128)} %bitcast.6, s32[32,128]{1,0:T(8,128)} %bitcast.8, bf16[32,128]{1,0:T(8,128)(2,1)} %bitcast.9, bf16[8,32,2048]{2,1,0:T(8,128)(2,1)} %echoes_in.1), custom_call_target="tpu_custom_call" | custom-call | tf_op jit(solution)/shard_map/pallas_call | solution.py:220
  7.3 0.0 copy-start
  7.3 8.6 %all-to-all-start = ((f32[64,8,128]{2,1,0:T(8,128)}), f32[64,8,128]{2,1,0:T(8,128)S(1)}, u32[]{:S(2)}, u32[]{:S(2)}) async-start(f32[64,8,128]{2,1,0:T(8,128)} %shard_map.64), calls=%async_computation | async-start | bytes 524288 | tf_op jit(solution)/shard_map/all_to_all | solution.py:245
  16.5 8.6 %all-to-all-done = f32[64,8,128]{2,1,0:T(8,128)S(1)} async-done(((f32[64,8,128]{2,1,0:T(8,128)}), f32[64,8,128]{2,1,0:T(8,128)S(1)}, u32[]{:S(2)}, u32[]{:S(2)}) %all-to-all-start) | async-done | bytes 262176 | tf_op jit(solution)/shard_map/all_to_all | solution.py:245
  25.1 0.0 copy-done
  25.1 0.2 shard_map.65
  25.3 3.7 %collective-permute-start.1 = (f32[4,8,128]{2,1,0:T(8,128)S(1)}, f32[4,8,128]{2,1,0:T(8,128)S(1)}, u32[]{:S(2)}, u32[]{:S(2)}) collective-permute-start(f32[4,8,128]{2,1,0:T(8,128)S(1)} %get-tuple-element.14.refs_0_), channel_id=1, source_target_pairs={{0,64},{32,96},{64,0},{96,32},{1,65},{33,97},{65,1},{97,33},{2,66}... | collective-permute-start | bytes 49160 | tf_op jit(solution)/shard_map/ppermute | solution.py:259
  29.0 0.0 collective-permute-start
  29.0 1.7 %collective-permute-done.1.refs_2_ = f32[4,8,128]{2,1,0:T(8,128)S(1)} collective-permute-done((f32[4,8,128]{2,1,0:T(8,128)S(1)}, f32[4,8,128]{2,1,0:T(8,128)S(1)}, u32[]{:S(2)}, u32[]{:S(2)}) %collective-permute-start.1) | collective-permute-done | bytes 16416 | tf_op jit(solution)/shard_map/ppermute | solution.py:259
  30.7 0.0 collective-permute-start.2
  30.7 0.0 collective-permute-done.refs_1_
  30.7 1.2 %collective-permute-done.2.refs_3_ = f32[4,8,128]{2,1,0:T(8,128)S(1)} collective-permute-done((f32[4,8,128]{2,1,0:T(8,128)S(1)}, f32[4,8,128]{2,1,0:T(8,128)S(1)}, u32[]{:S(2)}, u32[]{:S(2)}) %collective-permute-start.2) | collective-permute-done | bytes 16416 | tf_op jit(solution)/shard_map/ppermute | solution.py:259
  31.9 0.3 shard_map.66
  32.2 0.0 copy-start.1
  32.2 12.2 %all_to_all.10.grams = f32[32,8,128]{2,1,0:T(8,128)S(1)} all-to-all(f32[32,8,128]{2,1,0:T(8,128)S(1)} %get-tuple-element.15), channel_id=1, replica_groups=mesh['frame'=4,'vox'=32] {'vox'}, dimensions={0} | all-to-all | bytes 262144 | tf_op jit(solution)/shard_map/all_to_all | solution.py:274
  44.4 0.0 copy-done.1
  44.4 0.1 broadcast_in_dim.2.start
  44.5 2.0 %shard_map.67 = f32[32,128]{1,0:T(8,128)} custom-call(f32[32,8,128]{2,1,0:T(8,128)S(1)} %all_to_all.10.grams, f32[32,128]{1,0:T(8,128)S(1)} %get-tuple-element.16.image, f32[16,32,128]{2,1,0:T(8,128)S(1)} %broadcast_in_dim.2.start, f32[16,128]{1,0:T(8,128)S(1)} %get-tuple-element.18.kept), custom_call_target="tpu_custom_call" | custom-call | tf_op jit(solution)/shard_map/pallas_call | solution.py:275
Async XLA Ops:
  7.3 17.9 %copy-start = (s32[128,32]{0,1:T(8,128)S(1)}, s32[128,32]{0,1:T(8,128)}, u32[]{:S(2)}) copy-start(s32[128,32]{0,1:T(8,128)} %param.9) | copy-start | bytes 49156
  7.3 17.8 %all-to-all-start = ((f32[64,8,128]{2,1,0:T(8,128)}), f32[64,8,128]{2,1,0:T(8,128)S(1)}, u32[]{:S(2)}, u32[]{:S(2)}) async-start(f32[64,8,128]{2,1,0:T(8,128)} %shard_map.64), calls=%async_computation | async-start | bytes 524288 | tf_op jit(solution)/shard_map/all_to_all | solution.py:245
  25.3 5.4 %collective-permute-start.1 = (f32[4,8,128]{2,1,0:T(8,128)S(1)}, f32[4,8,128]{2,1,0:T(8,128)S(1)}, u32[]{:S(2)}, u32[]{:S(2)}) collective-permute-start(f32[4,8,128]{2,1,0:T(8,128)S(1)} %get-tuple-element.14.refs_0_), channel_id=1, source_target_pairs={{0,64},{32,96},{64,0},{96,32},{1,65},{33,97},{65,1},{97,33},{2,66}... | collective-permute-start | bytes 49160 | tf_op jit(solution)/shard_map/ppermute | solution.py:259
  29.0 1.7 %collective-permute-start = (f32[4,8,128]{2,1,0:T(8,128)S(1)}, f32[4,8,128]{2,1,0:T(8,128)S(1)}, u32[]{:S(2)}, u32[]{:S(2)}) collective-permute-start(f32[4,8,128]{2,1,0:T(8,128)S(1)} %get-tuple-element.14.refs_0_), channel_id=1, source_target_pairs={{0,32},{32,0},{64,96},{96,64},{1,33},{33,1},{65,97},{97,65},{2,34}... | collective-permute-start | bytes 49160 | tf_op jit(solution)/shard_map/ppermute | solution.py:259
  30.7 1.2 %collective-permute-start.2 = (f32[4,8,128]{2,1,0:T(8,128)S(1)}, f32[4,8,128]{2,1,0:T(8,128)S(1)}, u32[]{:S(2)}, u32[]{:S(2)}) collective-permute-start(f32[4,8,128]{2,1,0:T(8,128)S(1)} %collective-permute-done.1.refs_2_), channel_id=1, source_target_pairs={{0,32},{32,0},{64,96},{96,64},{1,33},{33,1},{65,97},{97,65},{2,34}... | collective-permute-start | bytes 49160 | tf_op jit(solution)/shard_map/ppermute | solution.py:259
  32.2 12.2 %copy-start.1 = (f32[32,16]{0,1:T(8,128)S(1)}, f32[32,16]{0,1:T(8,128)}, u32[]{:S(2)}) copy-start(f32[32,16]{0,1:T(8,128)} %param.10) | copy-start | bytes 6148

commit v6 on v4

--- a/solution.py
+++ b/solution.py
@@ -8,6 +8,7 @@
 VB = 128
 SLOTS = 2
 STEP = 8
+REST = 2
 HIGHEST = lax.Precision.HIGHEST
 
 
@@ -45,10 +46,6 @@
         copies[part].start()
     copy_apod.start()
 
-    to_row = lax.broadcasted_iota(jnp.int32, (tile_rows, tile_rows), 0)
-    from_row = lax.broadcasted_iota(jnp.int32, (tile_rows, tile_rows), 1)
-    moves = (to_row & (f_dev - 1)) * group + lax.shift_right_logical(to_row, 3) == from_row
-    moves = jnp.where(moves, 1.0, 0.0).astype(raw.dtype)
     tiles[0:group] = jnp.zeros((group, f_dev, VB), jnp.float32)
 
     copy_delays.wait()
@@ -93,35 +90,43 @@
     for copy in copies:
         copy.wait()
 
-    for q in range(0, n_tiles, 2):
-        pair = raw[:, :, q * VB : (q + 2) * VB].reshape(tile_rows, 2 * VB)
-        pair = jnp.dot(moves, pair, preferred_element_type=jnp.float32)
-        for half in range(2):
-            tiles[(q + half + 1) * group : (q + half + 2) * group] = pair[
-                :, half * VB : (half + 1) * VB
-            ].reshape(group, f_dev, VB)
+    flat = tiles.reshape((n_tiles + 1) * tile_rows, VB)
+    for q in range(n_tiles):
+        for f in range(f_dev):
+            flat[pl.ds((q + 1) * tile_rows + f, group, stride=f_dev), :] = raw[
+                f, :, q * VB : (q + 1) * VB
+            ].astype(jnp.float32)
 
     put_rows.wait()
     put_turns.wait()
 
-    def step(s, carry):
-        half = s & 1
-        own = [blocks[s * STEP + i] for i in range(STEP)]
-        totals = [None] * STEP
+    def beam(base, size):
+        own = [blocks[base + i] for i in range(size)]
+        at = (base & (2 * STEP - 1)) * group
+        totals = [None] * size
         for e in range(group):
-            for i in range(STEP):
+            for i in range(size):
                 row = row_words[e, own[i]]
                 turn = turn_words[e, own[i]]
                 mixed = jnp.where(past <= turn, tiles[row], tiles[row + group])
-                weight = weight_wide[pl.ds((half * STEP + i) * group + e, 1), :]
+                weight = weight_wide[pl.ds(at + i * group + e, 1), :]
                 term = pltpu.roll(mixed, turn, 1) * weight
                 totals[i] = term if e == 0 else totals[i] + term
-        for i in range(STEP):
-            out[places[s * STEP + i]] = totals[i]
-        spread(s + 1, 1 - half)
+        for i in range(size):
+            out[places[base + i]] = totals[i]
+
+    def full_step(s, carry):
+        beam(s * STEP, STEP)
+        spread(s + 1, 1 - (s & 1))
         return carry
 
-    lax.fori_loop(0, (count + STEP - 1) // STEP, step, 0)
+    def rest_step(t, carry):
+        beam(full * STEP + t * REST, REST)
+        return carry
+
+    full = count // STEP
+    lax.fori_loop(0, full, full_step, 0)
+    lax.fori_loop(0, (count - full * STEP + REST - 1) // REST, rest_step, 0)
 
 
 def place_kernel(rank, marks, parts, out, kept, picks):

time: 46.7 us -> 46.2 us (0.989)
  no operation moved by 1% of the time
where the time goes in v6:
time: 46.2 us; the launch traced here: 46 us
  starting transfers between devices  12.4 us (27%)
  blocking collectives  12.2 us (26%)
  waiting for transfers between devices  11.5 us (25%)
  Pallas kernels  8.99 us (19%)
  between operations  0.71 us (2%)
    all_to_all x1, blocking collectives, per_device(): lax.all_to_all(grams, 'vox', split_axis=0, concat_axis=0, tiled=True)  12.2 us
    all_to_all x1, starting transfers between devices, per_device(): lax.all_to_all(slots, 'vox', split_axis=0, concat_axis=0, tiled=True)  8.77 us
    all_to_all x1, waiting for transfers between devices, per_device(): lax.all_to_all(slots, 'vox', split_axis=0, concat_axis=0, tiled=True)  8.6 us
    pallas_call x1, Pallas kernels, per_device(): pl.pallas_call(beam_kernel, out_shape=jax.ShapeDtypeStruct((n_vox * SLOTS...  6.57 us
    ppermute x3, starting transfers between devices, flipped(): return lax.ppermute(value, 'frame', [(f, f ^ flip) for f in range(n_frame)])  3.67 us
    ppermute x3, waiting for transfers between devices, flipped(): return lax.ppermute(value, 'frame', [(f, f ^ flip) for f in range(n_frame)])  2.9 us
    pallas_call x1, Pallas kernels, per_device(): pl.pallas_call(subspace_kernel, out_shape=jax.ShapeDtypeStruct((frames, V...  1.98 us
  transfers between devices with their start and end apart: 4, of which 3 were waited for; matrix products, arithmetic and copies ran while one was open for 0% of the time, Pallas kernels for 0%

profile of v6, /device:TPU:0, one launch (start us, length us, event | category | flops | bytes accessed | tf_op | source)
XLA Modules:
  0.0 46.0 jit_solution(399852815277815495)
XLA Ops:
  0.0 6.6 %shard_map.64 = f32[64,8,128]{2,1,0:T(8,128)} custom-call(s32[32,128]{1,0:T(8,128)} %bitcast.6, s32[32,128]{1,0:T(8,128)} %bitcast.8, bf16[32,128]{1,0:T(8,128)(2,1)} %bitcast.9, bf16[8,32,2048]{2,1,0:T(8,128)(2,1)} %echoes_in.1), custom_call_target="tpu_custom_call" | custom-call | tf_op jit(solution)/shard_map/pallas_call | solution.py:223
  6.6 0.0 copy-start
  6.6 8.8 %all-to-all-start = ((f32[64,8,128]{2,1,0:T(8,128)}), f32[64,8,128]{2,1,0:T(8,128)S(1)}, u32[]{:S(2)}, u32[]{:S(2)}) async-start(f32[64,8,128]{2,1,0:T(8,128)} %shard_map.64), calls=%async_computation | async-start | bytes 524288 | tf_op jit(solution)/shard_map/all_to_all | solution.py:248
  16.0 8.6 %all-to-all-done = f32[64,8,128]{2,1,0:T(8,128)S(1)} async-done(((f32[64,8,128]{2,1,0:T(8,128)}), f32[64,8,128]{2,1,0:T(8,128)S(1)}, u32[]{:S(2)}, u32[]{:S(2)}) %all-to-all-start) | async-done | bytes 262176 | tf_op jit(solution)/shard_map/all_to_all | solution.py:248
  24.6 0.0 copy-done
  24.6 0.2 shard_map.65
  24.8 3.7 %collective-permute-start.1 = (f32[4,8,128]{2,1,0:T(8,128)S(1)}, f32[4,8,128]{2,1,0:T(8,128)S(1)}, u32[]{:S(2)}, u32[]{:S(2)}) collective-permute-start(f32[4,8,128]{2,1,0:T(8,128)S(1)} %get-tuple-element.14.refs_0_), channel_id=1, source_target_pairs={{0,64},{32,96},{64,0},{96,32},{1,65},{33,97},{65,1},{97,33},{2,66}... | collective-permute-start | bytes 49160 | tf_op jit(solution)/shard_map/ppermute | solution.py:262
  28.4 0.0 collective-permute-start
  28.5 1.7 %collective-permute-done.1.refs_2_ = f32[4,8,128]{2,1,0:T(8,128)S(1)} collective-permute-done((f32[4,8,128]{2,1,0:T(8,128)S(1)}, f32[4,8,128]{2,1,0:T(8,128)S(1)}, u32[]{:S(2)}, u32[]{:S(2)}) %collective-permute-start.1) | collective-permute-done | bytes 16416 | tf_op jit(solution)/shard_map/ppermute | solution.py:262
  30.2 0.0 collective-permute-start.2
  30.2 0.0 collective-permute-done.refs_1_
  30.2 1.2 %collective-permute-done.2.refs_3_ = f32[4,8,128]{2,1,0:T(8,128)S(1)} collective-permute-done((f32[4,8,128]{2,1,0:T(8,128)S(1)}, f32[4,8,128]{2,1,0:T(8,128)S(1)}, u32[]{:S(2)}, u32[]{:S(2)}) %collective-permute-start.2) | collective-permute-done | bytes 16416 | tf_op jit(solution)/shard_map/ppermute | solution.py:262
  31.4 0.3 shard_map.66
  31.6 0.0 copy-start.1
  31.7 12.2 %all_to_all.10.grams = f32[32,8,128]{2,1,0:T(8,128)S(1)} all-to-all(f32[32,8,128]{2,1,0:T(8,128)S(1)} %get-tuple-element.15), channel_id=1, replica_groups=mesh['frame'=4,'vox'=32] {'vox'}, dimensions={0} | all-to-all | bytes 262144 | tf_op jit(solution)/shard_map/all_to_all | solution.py:277
  43.9 0.0 copy-done.1
  43.9 0.1 broadcast_in_dim.2.start
  44.0 2.0 %shard_map.67 = f32[32,128]{1,0:T(8,128)} custom-call(f32[32,8,128]{2,1,0:T(8,128)S(1)} %all_to_all.10.grams, f32[32,128]{1,0:T(8,128)S(1)} %get-tuple-element.16.image, f32[16,32,128]{2,1,0:T(8,128)S(1)} %broadcast_in_dim.2.start, f32[16,128]{1,0:T(8,128)S(1)} %get-tuple-element.18.kept), custom_call_target="tpu_custom_call" | custom-call | tf_op jit(solution)/shard_map/pallas_call | solution.py:278
Async XLA Ops:
  6.6 18.0 %copy-start = (s32[128,32]{0,1:T(8,128)S(1)}, s32[128,32]{0,1:T(8,128)}, u32[]{:S(2)}) copy-start(s32[128,32]{0,1:T(8,128)} %param.9) | copy-start | bytes 49156
  6.6 18.0 %all-to-all-start = ((f32[64,8,128]{2,1,0:T(8,128)}), f32[64,8,128]{2,1,0:T(8,128)S(1)}, u32[]{:S(2)}, u32[]{:S(2)}) async-start(f32[64,8,128]{2,1,0:T(8,128)} %shard_map.64), calls=%async_computation | async-start | bytes 524288 | tf_op jit(solution)/shard_map/all_to_all | solution.py:248
  24.8 5.4 %collective-permute-start.1 = (f32[4,8,128]{2,1,0:T(8,128)S(1)}, f32[4,8,128]{2,1,0:T(8,128)S(1)}, u32[]{:S(2)}, u32[]{:S(2)}) collective-permute-start(f32[4,8,128]{2,1,0:T(8,128)S(1)} %get-tuple-element.14.refs_0_), channel_id=1, source_target_pairs={{0,64},{32,96},{64,0},{96,32},{1,65},{33,97},{65,1},{97,33},{2,66}... | collective-permute-start | bytes 49160 | tf_op jit(solution)/shard_map/ppermute | solution.py:262
  28.4 1.7 %collective-permute-start = (f32[4,8,128]{2,1,0:T(8,128)S(1)}, f32[4,8,128]{2,1,0:T(8,128)S(1)}, u32[]{:S(2)}, u32[]{:S(2)}) collective-permute-start(f32[4,8,128]{2,1,0:T(8,128)S(1)} %get-tuple-element.14.refs_0_), channel_id=1, source_target_pairs={{0,32},{32,0},{64,96},{96,64},{1,33},{33,1},{65,97},{97,65},{2,34}... | collective-permute-start | bytes 49160 | tf_op jit(solution)/shard_map/ppermute | solution.py:262
  30.2 1.2 %collective-permute-start.2 = (f32[4,8,128]{2,1,0:T(8,128)S(1)}, f32[4,8,128]{2,1,0:T(8,128)S(1)}, u32[]{:S(2)}, u32[]{:S(2)}) collective-permute-start(f32[4,8,128]{2,1,0:T(8,128)S(1)} %collective-permute-done.1.refs_2_), channel_id=1, source_target_pairs={{0,32},{32,0},{64,96},{96,64},{1,33},{33,1},{65,97},{97,65},{2,34}... | collective-permute-start | bytes 49160 | tf_op jit(solution)/shard_map/ppermute | solution.py:262
  31.6 12.2 %copy-start.1 = (f32[32,16]{0,1:T(8,128)S(1)}, f32[32,16]{0,1:T(8,128)}, u32[]{:S(2)}) copy-start(f32[32,16]{0,1:T(8,128)} %param.10) | copy-start | bytes 6148

commit v7 on v6

--- a/solution.py
+++ b/solution.py
@@ -76,7 +76,8 @@
         blocks[count + i] = blocks[count - 1]
         places[count + i] = places[count - 1]
 
-    past = VB - lax.broadcasted_iota(jnp.int32, (f_dev, VB), 1)
+    lane = lax.broadcasted_iota(jnp.int32, (f_dev, VB), 1)
+    past = VB - lane
     block_row = lax.broadcasted_iota(jnp.int32, (n_blocks, VB), 0)
 
     def spread(s, half):
@@ -110,7 +111,10 @@
                 turn = turn_words[e, own[i]]
                 mixed = jnp.where(past <= turn, tiles[row], tiles[row + group])
                 weight = weight_wide[pl.ds(at + i * group + e, 1), :]
-                term = pltpu.roll(mixed, turn, 1) * weight
+                if e % 4 == 3:
+                    term = turned(mixed, (lane - turn) & (VB - 1)) * weight
+                else:
+                    term = pltpu.roll(mixed, turn, 1) * weight
                 totals[i] = term if e == 0 else totals[i] + term
         for i in range(size):
             out[places[base + i]] = totals[i]

time: 46.2 us -> 46.6 us (level)
  no operation moved by 1% of the time
where the time goes in v7:
time: 46.6 us; the launch traced here: 46.2 us
  starting transfers between devices  12.4 us (27%)
  blocking collectives  12.2 us (26%)
  waiting for transfers between devices  11.5 us (25%)
  Pallas kernels  9.19 us (20%)
  between operations  0.71 us (2%)
    all_to_all x1, blocking collectives, per_device(): lax.all_to_all(grams, 'vox', split_axis=0, concat_axis=0, tiled=True)  12.2 us
    all_to_all x1, starting transfers between devices, per_device(): lax.all_to_all(slots, 'vox', split_axis=0, concat_axis=0, tiled=True)  8.77 us
    all_to_all x1, waiting for transfers between devices, per_device(): lax.all_to_all(slots, 'vox', split_axis=0, concat_axis=0, tiled=True)  8.6 us
    pallas_call x1, Pallas kernels, per_device(): pl.pallas_call(beam_kernel, out_shape=jax.ShapeDtypeStruct((n_vox * SLOTS...  6.78 us
    ppermute x3, starting transfers between devices, flipped(): return lax.ppermute(value, 'frame', [(f, f ^ flip) for f in range(n_frame)])  3.67 us
    ppermute x3, waiting for transfers between devices, flipped(): return lax.ppermute(value, 'frame', [(f, f ^ flip) for f in range(n_frame)])  2.9 us
    pallas_call x1, Pallas kernels, per_device(): pl.pallas_call(subspace_kernel, out_shape=jax.ShapeDtypeStruct((frames, V...  1.97 us
  transfers between devices with their start and end apart: 4, of which 3 were waited for; matrix products, arithmetic and copies ran while one was open for 0% of the time, Pallas kernels for 0%

profile of v7, /device:TPU:0, one launch (start us, length us, event | category | flops | bytes accessed | tf_op | source)
XLA Modules:
  0.0 46.2 jit_solution(4999355579607724665)
XLA Ops:
  0.0 6.8 %shard_map.64 = f32[64,8,128]{2,1,0:T(8,128)} custom-call(s32[32,128]{1,0:T(8,128)} %bitcast.6, s32[32,128]{1,0:T(8,128)} %bitcast.8, bf16[32,128]{1,0:T(8,128)(2,1)} %bitcast.9, bf16[8,32,2048]{2,1,0:T(8,128)(2,1)} %echoes_in.1), custom_call_target="tpu_custom_call" | custom-call | tf_op jit(solution)/shard_map/pallas_call | solution.py:227
  6.8 0.0 copy-start
  6.8 8.8 %all-to-all-start = ((f32[64,8,128]{2,1,0:T(8,128)}), f32[64,8,128]{2,1,0:T(8,128)S(1)}, u32[]{:S(2)}, u32[]{:S(2)}) async-start(f32[64,8,128]{2,1,0:T(8,128)} %shard_map.64), calls=%async_computation | async-start | bytes 524288 | tf_op jit(solution)/shard_map/all_to_all | solution.py:252
  16.2 8.6 %all-to-all-done = f32[64,8,128]{2,1,0:T(8,128)S(1)} async-done(((f32[64,8,128]{2,1,0:T(8,128)}), f32[64,8,128]{2,1,0:T(8,128)S(1)}, u32[]{:S(2)}, u32[]{:S(2)}) %all-to-all-start) | async-done | bytes 262176 | tf_op jit(solution)/shard_map/all_to_all | solution.py:252
  24.8 0.0 copy-done
  24.8 0.2 shard_map.65
  25.0 3.7 %collective-permute-start.1 = (f32[4,8,128]{2,1,0:T(8,128)S(1)}, f32[4,8,128]{2,1,0:T(8,128)S(1)}, u32[]{:S(2)}, u32[]{:S(2)}) collective-permute-start(f32[4,8,128]{2,1,0:T(8,128)S(1)} %get-tuple-element.14.refs_0_), channel_id=1, source_target_pairs={{0,64},{32,96},{64,0},{96,32},{1,65},{33,97},{65,1},{97,33},{2,66}... | collective-permute-start | bytes 49160 | tf_op jit(solution)/shard_map/ppermute | solution.py:266
  28.7 0.0 collective-permute-start
  28.7 1.7 %collective-permute-done.1.refs_2_ = f32[4,8,128]{2,1,0:T(8,128)S(1)} collective-permute-done((f32[4,8,128]{2,1,0:T(8,128)S(1)}, f32[4,8,128]{2,1,0:T(8,128)S(1)}, u32[]{:S(2)}, u32[]{:S(2)}) %collective-permute-start.1) | collective-permute-done | bytes 16416 | tf_op jit(solution)/shard_map/ppermute | solution.py:266
  30.4 0.0 collective-permute-start.2
  30.4 0.0 collective-permute-done.refs_1_
  30.4 1.2 %collective-permute-done.2.refs_3_ = f32[4,8,128]{2,1,0:T(8,128)S(1)} collective-permute-done((f32[4,8,128]{2,1,0:T(8,128)S(1)}, f32[4,8,128]{2,1,0:T(8,128)S(1)}, u32[]{:S(2)}, u32[]{:S(2)}) %collective-permute-start.2) | collective-permute-done | bytes 16416 | tf_op jit(solution)/shard_map/ppermute | solution.py:266
  31.6 0.3 shard_map.66
  31.9 0.0 copy-start.1
  31.9 12.2 %all_to_all.10.grams = f32[32,8,128]{2,1,0:T(8,128)S(1)} all-to-all(f32[32,8,128]{2,1,0:T(8,128)S(1)} %get-tuple-element.15), channel_id=1, replica_groups=mesh['frame'=4,'vox'=32] {'vox'}, dimensions={0} | all-to-all | bytes 262144 | tf_op jit(solution)/shard_map/all_to_all | solution.py:281
  44.1 0.0 copy-done.1
  44.1 0.1 broadcast_in_dim.2.start
  44.2 2.0 %shard_map.67 = f32[32,128]{1,0:T(8,128)} custom-call(f32[32,8,128]{2,1,0:T(8,128)S(1)} %all_to_all.10.grams, f32[32,128]{1,0:T(8,128)S(1)} %get-tuple-element.16.image, f32[16,32,128]{2,1,0:T(8,128)S(1)} %broadcast_in_dim.2.start, f32[16,128]{1,0:T(8,128)S(1)} %get-tuple-element.18.kept), custom_call_target="tpu_custom_call" | custom-call | tf_op jit(solution)/shard_map/pallas_call | solution.py:282
Async XLA Ops:
  6.8 18.0 %copy-start = (s32[128,32]{0,1:T(8,128)S(1)}, s32[128,32]{0,1:T(8,128)}, u32[]{:S(2)}) copy-start(s32[128,32]{0,1:T(8,128)} %param.9) | copy-start | bytes 49156
  6.8 18.0 %all-to-all-start = ((f32[64,8,128]{2,1,0:T(8,128)}), f32[64,8,128]{2,1,0:T(8,128)S(1)}, u32[]{:S(2)}, u32[]{:S(2)}) async-start(f32[64,8,128]{2,1,0:T(8,128)} %shard_map.64), calls=%async_computation | async-start | bytes 524288 | tf_op jit(solution)/shard_map/all_to_all | solution.py:252
  25.0 5.4 %collective-permute-start.1 = (f32[4,8,128]{2,1,0:T(8,128)S(1)}, f32[4,8,128]{2,1,0:T(8,128)S(1)}, u32[]{:S(2)}, u32[]{:S(2)}) collective-permute-start(f32[4,8,128]{2,1,0:T(8,128)S(1)} %get-tuple-element.14.refs_0_), channel_id=1, source_target_pairs={{0,64},{32,96},{64,0},{96,32},{1,65},{33,97},{65,1},{97,33},{2,66}... | collective-permute-start | bytes 49160 | tf_op jit(solution)/shard_map/ppermute | solution.py:266
  28.7 1.7 %collective-permute-start = (f32[4,8,128]{2,1,0:T(8,128)S(1)}, f32[4,8,128]{2,1,0:T(8,128)S(1)}, u32[]{:S(2)}, u32[]{:S(2)}) collective-permute-start(f32[4,8,128]{2,1,0:T(8,128)S(1)} %get-tuple-element.14.refs_0_), channel_id=1, source_target_pairs={{0,32},{32,0},{64,96},{96,64},{1,33},{33,1},{65,97},{97,65},{2,34}... | collective-permute-start | bytes 49160 | tf_op jit(solution)/shard_map/ppermute | solution.py:266
  30.4 1.2 %collective-permute-start.2 = (f32[4,8,128]{2,1,0:T(8,128)S(1)}, f32[4,8,128]{2,1,0:T(8,128)S(1)}, u32[]{:S(2)}, u32[]{:S(2)}) collective-permute-start(f32[4,8,128]{2,1,0:T(8,128)S(1)} %collective-permute-done.1.refs_2_), channel_id=1, source_target_pairs={{0,32},{32,0},{64,96},{96,64},{1,33},{33,1},{65,97},{97,65},{2,34}... | collective-permute-start | bytes 49160 | tf_op jit(solution)/shard_map/ppermute | solution.py:266
  31.9 12.2 %copy-start.1 = (f32[32,16]{0,1:T(8,128)S(1)}, f32[32,16]{0,1:T(8,128)}, u32[]{:S(2)}) copy-start(f32[32,16]{0,1:T(8,128)} %param.10) | copy-start | bytes 6148
